TPU v7x, 512 devices: a whole 4x8x8 slice. The times are simulated.
512 devices in a mesh: dp: 32 (over y, x_lo, core), shard: 16 (over z, x_hi).
Axes of the slice: x: 4 (x_hi: 2, x_lo: 2; x = x_hi * 2 + x_lo), y: 8, z: 8, core: 2. Of those that a mesh axis runs over, the one named last changes fastest.
Arguments:
- residual: bfloat16 [16384, 8192], P('shard', 'dp'), may hold values from -66 to 66
- norm_gain: float32 [8192], P('shard'), may hold values from 0.5 to 2
- value_weight: bfloat16 [8192, 512], P('shard'), may hold values from -0.0625 to 0.0625
- rotation: float32 [8192, 8192], P('shard', 'dp'), may hold values from -1.3 to 1.3
- target: bfloat16 [16384, 512], P('shard'), may hold values from -6 to 6
Outputs:
- grad_rotation: float32 [8192, 8192], P('shard', 'dp')
- rotation_next: float32 [8192, 8192], P('shard', 'dp')
All inputs are finite; a program needn't handle non-finite values. Where the computation divides by a largest or mean magnitude, that divisor is 1e-20 or more.
Results may differ from a plain program's by a relative error of at most 0.0039.
Values may be sent and summed in bfloat16 or wider, within the bound.
A program may use at most 64 MiB of HBM per device.

v0:
```python
import math

import jax
import jax.numpy as jnp
from jax import lax
from jax.sharding import PartitionSpec as P

D = 8192


two_pi = 2.0 * math.pi
precise = lax.Precision.HIGHEST


def soft_round(values):
    return values - jnp.sin(two_pi * values) / two_pi


def shards(residual, norm_gain, value_weight, rotation, target):
    hidden = residual.astype(jnp.float32)
    local_square = jnp.sum(hidden * hidden, axis=1)
    local_peak = jnp.max(jnp.abs(hidden), axis=1)
    row_square = lax.psum(local_square, "dp")
    row_top = lax.pmax(local_peak, "dp")
    inv_rms = lax.rsqrt(row_square[:, None] / D + 1e-05)
    row_peak = row_top[:, None] + 1e-06
    act_quant = (row_peak * inv_rms / 7.0 * soft_round(7.0 * hidden / row_peak)).astype(
        jnp.bfloat16
    )
    scaled_weight = norm_gain[:, None] * value_weight.astype(jnp.float32) / math.sqrt(D)
    rotated = lax.psum(jnp.dot(rotation.T, scaled_weight, precision=precise), "shard")
    column_peak = lax.pmax(jnp.max(jnp.abs(rotated), axis=0), "dp")
    weight_scale = (column_peak[None, :] + 1e-06) / 7.0
    weight_quant = (weight_scale * soft_round(rotated / weight_scale)).astype(jnp.bfloat16)
    share_rows = act_quant.shape[0] // lax.axis_size("dp")
    value_width = value_weight.shape[1]
    rows_block = act_quant
    outputs = lax.psum_scatter(
        jnp.dot(rows_block, weight_quant, preferred_element_type=jnp.float32),
        "dp",
        scatter_dimension=0,
        tiled=True,
    )
    target_rows = lax.dynamic_slice_in_dim(target, lax.axis_index("dp") * share_rows, share_rows, 0)
    out_grad = (outputs - target_rows.astype(jnp.float32)).astype(jnp.bfloat16)
    rows_block = act_quant
    partial_grad = jnp.einsum(
        "tj,tk->jk",
        rows_block,
        lax.all_gather(out_grad, "dp", axis=0, tiled=True),
        preferred_element_type=jnp.float32,
    )
    weight_grad = lax.psum(partial_grad, "shard")
    grad_rotation = jnp.dot(scaled_weight, weight_grad.T, precision=precise)
    local_norm = jnp.sum(grad_rotation * grad_rotation)
    grad_part = jnp.dot(rotation, weight_grad, precision=precise)
    grad_square = lax.psum(local_norm, ("dp", "shard"))
    rotated_grad = lax.psum(grad_part, "dp")
    first_part = jnp.dot(rotated_grad.T, rotation, precision=precise)
    first_terms = lax.psum(first_part.astype(jnp.bfloat16), "shard").astype(jnp.float32)
    step_size = 0.4 * math.sqrt(value_width) / jnp.sqrt(D * grad_square + 1e-06)
    first_step = jnp.dot(scaled_weight, first_terms, precision=precise) - jnp.dot(
        rotated_grad, rotated.T, precision=precise
    )
    current = rotation - step_size * first_step
    summed = rotation + current
    left_part = jnp.dot(rotated_grad.T, summed, precision=precise)
    right_part = jnp.dot(scaled_weight.T, summed, precision=precise)
    left_terms, right_terms = lax.psum((left_part, right_part), "shard")
    applied = jnp.dot(scaled_weight, left_terms, precision=precise) - jnp.dot(
        rotated_grad, right_terms, precision=precise
    )
    current = rotation - 0.5 * step_size * applied
    return (grad_rotation, current)


def solution(mesh):
    in_specs = (P("shard", "dp"), P("shard"), P("shard", None), P("shard", "dp"), P("shard", None))
    out_specs = (P("shard", "dp"), P("shard", "dp"))
    return jax.shard_map(shards, mesh=mesh, in_specs=in_specs, out_specs=out_specs, check_vma=False)
```

profile of v0, /device:TPU:1, one launch (start us, length us, event | category | flops | bytes accessed | tf_op | source)
XLA Modules:
  0.0 1178.6 jit_solution(12979441679170052009)
XLA Ops:
  7.2 0.0 all-reduce.8.cloned.1.call-start
  7.2 4.0 convolution_bitcast_fusion.1
  11.2 0.0 reduce-scatter.2.cloned.1.call-start
  11.3 0.4 fusion.6
  11.7 59.8 %psum.56 = f32[1024]{0:T(1024)S(1)} all-reduce(f32[1024]{0:T(1024)S(1)} %get-tuple-element.2), channel_id=1, replica_groups=mesh['dp'=32,'shard'=16] {'dp'}, use_global_device_ids=true, to_apply=%region_3.0 | all-reduce | flops 1024 | bytes 8192 | tf_op jit(solution)/shard_map/psum | solution.py:23
  71.4 100.1 %all-reduce.8.cloned.1.call-done = f32[256,512]{0,1:T(8,128)} async-done(((f32[256,512]{0,1:T(8,128)}), f32[256,512]{0,1:T(8,128)}) %all-reduce.8.cloned.1.call-update) | async-done | bytes 524304 | tf_op jit(solution)/shard_map/psum | solution.py:31
  171.5 1.2 abs_reduce_fusion
  172.7 63.8 %all-reduce = (f32[512]{0:T(512)S(1)}, f32[1024]{0:T(1024)S(1)}) all-reduce(f32[512]{0:T(512)S(1)} %abs_reduce_fusion, f32[1024]{0:T(1024)S(1)} %get-tuple-element.3), channel_id=1, replica_groups=mesh['dp'=32,'shard'=16] {'dp'}, use_global_device_ids=true, to_apply=%region_6.0 | all-reduce | flops 1536 | bytes 12288 | tf_op jit(solution)/shard_map/pmax | solution.py:32
  236.5 8.1 fusion.22
  244.7 0.0 all-gather.2.cloned.1.call-start
  244.7 116.0 %reduce-scatter.2.cloned.1.call-done = f32[32,512]{1,0:T(8,128)} async-done(((f32[1024,512]{1,0:T(8,128)}), f32[32,512]{1,0:T(8,128)}) %reduce-scatter.2.cloned.1.call-update) | async-done | bytes 65552 | tf_op jit(solution)/shard_map/reduce_scatter | solution.py:38
  360.7 1.5 subtract_convert_fusion
  362.2 0.2 all-reduce.10.cloned.1.call-start
  362.4 68.9 %all-gather.2.cloned.1.call-done = bf16[1024,512]{1,0:T(8,128)(2,1)} async-done(((bf16[32,512]{1,0:T(8,128)(2,1)}), bf16[1024,512]{1,0:T(8,128)(2,1)}) %all-gather.2.cloned.1.call-update) | async-done | bytes 1048592 | tf_op jit(solution)/shard_map/all_gather | solution.py:50
  431.3 6.1 fusion.33
  437.5 0.0 all-reduce.12.cloned.1.call-start
  437.5 154.1 %all-reduce.10.cloned.1.call-done = f32[256,512]{1,0:T(8,128)} async-done(((f32[256,512]{1,0:T(8,128)}), f32[256,512]{1,0:T(8,128)}) %all-reduce.10.cloned.1.call-update) | async-done | bytes 524304 | tf_op jit(solution)/shard_map/psum | solution.py:53
  591.6 3.9 convolution_bitcast_fusion
  595.6 0.0 all-reduce.14.cloned.1.call-start
  595.6 240.1 %all-reduce.12.cloned.1.call-done = f32[512,512]{0,1:T(8,128)} async-done(((f32[512,512]{0,1:T(8,128)}), f32[512,512]{0,1:T(8,128)}) %all-reduce.12.cloned.1.call-update) | async-done | bytes 1048592 | tf_op jit(solution)/shard_map/psum | solution.py:58
  835.7 3.0 convolution_convert_fusion
  838.7 0.0 all-reduce.16.cloned.1.call-start
  838.8 2.5 multiply_reduce_fusion
  841.3 101.1 %psum.59 = f32[]{:T(128)} all-reduce(f32[]{:T(128)} %get-tuple-element.10), channel_id=1, replica_groups=mesh['dp'=32,'shard'=16] {'dp','shard'}, use_global_device_ids=true, to_apply=%region_10.0 | all-reduce | flops 1 | bytes 8 | tf_op jit(solution)/shard_map/psum | solution.py:57
  943.1 50.0 %all-reduce.14.cloned.1.call-done = bf16[512,256]{1,0:T(8,128)(2,1)} async-done(((bf16[512,256]{1,0:T(8,128)(2,1)}), bf16[512,256]{1,0:T(8,128)(2,1)}) %all-reduce.14.cloned.1.call-update) | async-done | bytes 262160 | tf_op jit(solution)/shard_map/psum | solution.py:60
  993.2 1.7 fusion.10
  994.9 1.8 fusion.4
  996.7 2.8 fusion.8
  999.5 1.8 fusion.34
  1001.3 164.6 %all-reduce.16.cloned.1.call-done = (f32[512,256]{1,0:T(8,128)}, f32[512,256]{1,0:T(8,128)}) async-done(((f32[512,256]{1,0:T(8,128)}, f32[512,256]{1,0:T(8,128)}), (f32[512,256]{1,0:T(8,128)}, f32[512,256]{1,0:T(8,128)})) %all-reduce.16.cloned.1.call-update) | async-done | bytes 1048592 | tf_op jit(solution)/shard_map/psum | solution.py:69
  1165.9 2.1 fusion.9
  1168.1 3.7 fusion.2
  (23 shorter events, 0.2 us)
Async XLA Ops:
  7.2 4.1 copy-start.5
  7.2 164.3 %all-reduce.8.cloned.1.call-start = ((), (), s32[]{:S(2)}) async-start(), calls=%async_computation.1 | async-start | bytes 1048576 | tf_op jit(solution)/shard_map/psum | solution.py:31
  11.2 349.4 %reduce-scatter.2.cloned.1.call-start = ((), (), s32[]{:S(2)}) async-start(), calls=%async_computation.2 | async-start | bytes 2162688 | tf_op jit(solution)/shard_map/reduce_scatter | solution.py:38
  244.7 186.6 %all-gather.2.cloned.1.call-start = ((), (), s32[]{:S(2)}) async-start(), calls=%async_computation.3 | async-start | bytes 1081344 | tf_op jit(solution)/shard_map/all_gather | solution.py:50
  362.2 229.4 %copy-start.2 = (f32[512,256]{1,0:T(8,128)S(1)}, f32[512,256]{1,0:T(8,128)}, u32[]{:S(2)}) copy-start(f32[512,256]{1,0:T(8,128)} %param.8) | copy-start | bytes 1572868
  362.2 229.4 %all-reduce.10.cloned.1.call-start = ((), (), s32[]{:S(2)}) async-start(), calls=%async_computation.4 | async-start | bytes 1048576 | tf_op jit(solution)/shard_map/psum | solution.py:53
  437.5 398.2 %all-reduce.12.cloned.1.call-start = ((), (), s32[]{:S(2)}) async-start(), calls=%async_computation.5 | async-start | bytes 2097152 | tf_op jit(solution)/shard_map/psum | solution.py:58
  595.5 243.2 %copy-start.1 = (bf16[512,512]{1,0:T(8,128)(2,1)S(1)}, bf16[512,512]{1,0:T(8,128)(2,1)}, u32[]{:S(2)}) copy-start(bf16[512,512]{1,0:T(8,128)(2,1)} %param.7) | copy-start | bytes 1572868
  595.5 243.2 %copy-start.3 = (f32[256,512]{1,0:T(8,128)S(1)}, f32[256,512]{1,0:T(8,128)}, u32[]{:S(2)}) copy-start(f32[256,512]{1,0:T(8,128)} %all-reduce.10.cloned.1.call-done) | copy-start | bytes 1572868
  595.5 243.2 %copy-start.6 = (f32[512]{0:T(512)S(1)}, f32[512]{0:T(512)}, u32[]{:S(2)}) copy-start(f32[512]{0:T(512)} %param.6) | copy-start | bytes 6148
  595.6 399.3 %copy-start.4 = (f32[256,512]{0,1:T(8,128)S(1)}, f32[256,512]{0,1:T(8,128)}, u32[]{:S(2)}) copy-start(f32[256,512]{0,1:T(8,128)} %all-reduce.8.cloned.1.call-done) | copy-start | bytes 1572868
  595.6 397.6 %all-reduce.14.cloned.1.call-start = ((), (), s32[]{:S(2)}) async-start(), calls=%async_computation.6 | async-start | bytes 524288 | tf_op jit(solution)/shard_map/psum | solution.py:60
  835.7 159.2 %copy-start = (f32[512,512]{0,1:T(8,128)S(1)}, f32[512,512]{0,1:T(8,128)}, u32[]{:S(2)}) copy-start(f32[512,512]{0,1:T(8,128)} %all-reduce.12.cloned.1.call-done) | copy-start | bytes 3145732
  838.7 327.2 %all-reduce.16.cloned.1.call-start = ((), (), s32[]{:S(2)}) async-start(), calls=%async_computation.7 | async-start | bytes 2097152 | tf_op jit(solution)/shard_map/psum | solution.py:69
Sparse Core Ops, SparseCore 0:
  11.5 159.9 all-reduce.7
  244.8 115.8 reduce-scatter.1
  363.4 67.8 all-gather.1
  437.6 153.9 all-reduce.9
  595.7 239.9 all-reduce.11
  839.0 154.0 all-reduce.13
  1001.4 164.4 all-reduce.15
where the time goes:
time: 1190 us; the launch traced here: 1180 us
  waiting for transfers between devices  894 us (75%)
  blocking collectives  225 us (19%)
  matrix products  41.5 us (3%)
  between operations  14.9 us (1%)
    psum x1, waiting for transfers between devices, shards(): rotated_grad = lax.psum(grad_part, 'dp')  240 us
    psum x1, waiting for transfers between devices, shards(): left_terms, right_terms = lax.psum((left_part, right_part), 'shard')  165 us
    psum x1, waiting for transfers between devices, shards(): weight_grad = lax.psum(partial_grad, 'shard')  154 us
    reduce_scatter x1, waiting for transfers between devices, shards(): lax.psum_scatter(jnp.dot(rows_block, weight_quant, preferred_element_type...  116 us
    psum x1, blocking collectives, shards(): grad_square = lax.psum(local_norm, ('dp', 'shard'))  101 us
    psum x1, waiting for transfers between devices, shards(): lax.psum(jnp.dot(rotation.T, scaled_weight, precision=precise), 'shard')  100 us
    all_gather x1, waiting for transfers between devices, shards(): lax.all_gather(out_grad, 'dp', axis=0, tiled=True)  68.9 us
    pmax x1, blocking collectives, shards(): column_peak = lax.pmax(jnp.max(jnp.abs(rotated), axis=0), 'dp')  63.8 us
  transfers between devices with their start and end apart: 7, of which 7 were waited for; matrix products, arithmetic and copies ran while one was open for 0% of the time, Pallas kernels for 0%

commit v1 on v0

v1 whole, which is shorter than its diff:
```python
import math

import jax
import jax.numpy as jnp
from jax import lax
from jax.experimental import pallas as pl
from jax.experimental.pallas import tpu as pltpu
from jax.sharding import PartitionSpec as P

D = 8192
N = 16
MESH = pl.DeviceIdType.MESH
F32 = jnp.float32
BF16 = jnp.bfloat16
HIGHEST = lax.Precision.HIGHEST

SINE = (
    0.9999999944722865,
    -6.579735439437006,
    12.987842893121643,
    -12.207428862935943,
    6.687066146603468,
    -2.366367060643953,
    0.5091905906829214,
)

NN = (((1,), (0,)), ((), ()))
NT = (((1,), (1,)), ((), ()))
TN = (((0,), (0,)), ((), ()))


def dot(a, b, dims=NN, precision=None):
    return lax.dot_general(a, b, dims, precision=precision, preferred_element_type=F32)


def soft(v):
    r = v - jnp.floor(v + 0.5)
    s = r * r
    p = jnp.full_like(s, SINE[-1])
    for c in SINE[-2::-1]:
        p = p * s + c
    return v - r * p


def twin(a):
    return jnp.concatenate([a, a], axis=1)


(
    STAT_C, STAT_D, Q_R, PEAK_C, PEAK_D, W_G, Q_G, OUT_C, OUT_R, OG_G, OG_C, G_R, G_G, V_C, V_R, V_G, VC_C,
    P_R, P_G, SQ_C, SQ_D, SQ_S, U_R, U_G, UD_G, UD_C, M_R, M_G, MD_G, MD_C,
) = range(30)
COUNT = 30


def kernel(
    res, gain, weight, rot, target, grad_out, next_out,
    st, rb, act, stat, stat_c, stat_d,
    q_send, q_recv, q_all, w_all,
    peak, peak_c, peak_d,
    out_send, out_c, out_half, out_recv, og_all,
    g_send, g_recv, g_all,
    v_send, v_c, v_half, v_recv, v_all,
    p_send, p_recv, p_all,
    sq, sq_c, sq_d, sq_s,
    u_send, u_recv, u_part, u_all,
    m_send, m_recv, m_part, m_all,
    sends, recvs,
):
    dp, me = lax.axis_index("dp"), lax.axis_index("shard")
    chip, core = lax.div(dp, 2), lax.rem(dp, 2)
    other = 1 - core
    twin_id = (chip * 2 + other, me)

    def shard_id(k):
        return lax.rem(me + k, N)

    def chip_id(k):
        return lax.rem(chip + k, N)

    def shard_dev(k):
        return (dp, shard_id(k))

    def chip_dev(k):
        return (chip_id(k) * 2 + core, me)

    def each(body):
        def step(k, _):
            body(k)
            return 0

        lax.fori_loop(1, N, step, 0)

    def start(src, dst, which, device):
        pltpu.make_async_remote_copy(
            src_ref=src, dst_ref=dst, send_sem=sends.at[which], recv_sem=recvs.at[which],
            device_id=device, device_id_type=MESH,
        ).start()

    sent = []

    def arrived(ref, which):
        pltpu.make_async_copy(ref, ref, recvs.at[which]).wait()
        sent.append((ref, which))

    def scatter(src, dst, which, over_shard):
        def body(k):
            if over_shard:
                start(src.at[shard_id(k)], dst.at[k - 1], which, shard_dev(k))
            else:
                start(src.at[chip_id(k)], dst.at[k - 1], which, chip_dev(k))

        each(body)

    def spread(ref, dst, which, over_shard):
        def body(k):
            start(ref, dst, which, shard_dev(k) if over_shard else chip_dev(k))

        each(body)

    def to_twin(src, dst, which):
        start(src, dst, which, twin_id)

    def total(own, recv):
        acc = own.astype(F32)
        for k in range(N - 1):
            acc = acc + recv[k].astype(F32)
        return acc

    barrier = pltpu.get_barrier_semaphore()
    pl.semaphore_signal(barrier, inc=1, device_id=twin_id, device_id_type=MESH)

    def greet(k):
        pl.semaphore_signal(barrier, inc=1, device_id=shard_dev(k), device_id_type=MESH)
        pl.semaphore_signal(barrier, inc=1, device_id=chip_dev(k), device_id_type=MESH)

    each(greet)

    st[...] = weight[...].astype(F32).T * gain[...] * (1.0 / math.sqrt(D))
    q_send[...] = dot(st[...], rot[...], NN, HIGHEST).reshape(N, 32, 256)
    pl.semaphore_wait(barrier, 2 * N - 1)
    scatter(q_send, q_recv, Q_R, True)

    for k in range(8):
        h = res[128 * k : 128 * k + 128, :].astype(F32)
        a, b = h[:, :128], h[:, 128:]
        stat[k : k + 1, :] = jnp.sum((a * a + b * b).T, axis=0, keepdims=True)
        stat[8 + k : 9 + k, :] = jnp.max(
            jnp.maximum(jnp.abs(a), jnp.abs(b)).T, axis=0, keepdims=True
        )
    to_twin(stat, stat_c, STAT_C)
    rb[...] = rot[...].astype(BF16)
    slot = core * N + chip
    stb = st[...].astype(BF16)
    mine = st[pl.ds(pl.multiple_of(slot * 16, 16), 16), :].astype(BF16)
    u_gram = dot(mine, stb, NT)
    for h in range(2):
        for b in range(4):
            block = u_gram[8 * h : 8 * h + 8, 128 * b : 128 * b + 128]
            u_send[8 * h + b] = block
            u_send[8 * h + 4 + b] = block
    arrived(stat_c, STAT_C)

    def combine(a, b):
        return jnp.concatenate([a[:8] + b[:8], jnp.maximum(a[8:], b[8:])], axis=0)

    both = combine(stat[...], stat_c[...])
    stat_d[0] = both
    each(lambda k: start(stat_d.at[0], stat_d.at[k], STAT_D, chip_dev(k)))

    arrived(q_recv, Q_R)
    q_mine = total(q_send[me], q_recv)
    top = jnp.maximum(jnp.abs(q_mine[:, :128]), jnp.abs(q_mine[:, 128:]))
    top = jnp.max(jnp.concatenate([top] * 4, axis=0).T, axis=0, keepdims=True)
    peak[...] = jnp.broadcast_to(top, (8, 128))
    to_twin(peak, peak_c, PEAK_C)

    arrived(stat_d.at[pl.ds(1, N - 1)], STAT_D)
    for k in range(1, N):
        both = combine(both, stat_d[k])
    row_peak = both[8:] + 1e-06
    inv_rms = lax.rsqrt(both[:8] / D + 1e-05)
    rows_in = 7.0 / row_peak
    rows_out = row_peak * inv_rms / 7.0

    arrived(peak_c, PEAK_C)
    top = jnp.maximum(peak[...], peak_c[...])
    peak_d[0] = top
    each(lambda k: start(peak_d.at[0], peak_d.at[k], PEAK_D, chip_dev(k)))

    for k in range(8):
        into = twin(jnp.broadcast_to(rows_in[k : k + 1, :], (128, 128)).T)
        outof = twin(jnp.broadcast_to(rows_out[k : k + 1, :], (128, 128)).T)
        h = res[128 * k : 128 * k + 128, :].astype(F32)
        act[128 * k : 128 * k + 128, :] = (outof * soft(into * h)).astype(BF16)

    arrived(peak_d.at[pl.ds(1, N - 1)], PEAK_D)
    for k in range(1, N):
        top = jnp.maximum(top, peak_d[k])
    column = jnp.broadcast_to(top[:1, :], (128, 128)).T[:32, :]
    scale = twin((column + 1e-06) / 7.0)
    w_all[me] = (scale * soft(q_mine / scale)).astype(BF16)
    spread(w_all.at[me], w_all.at[me], W_G, True)
    q_all[me] = q_mine.astype(BF16)
    spread(q_all.at[me], q_all.at[me], Q_G, True)
    scatter(u_send, u_recv, U_R, True)

    wanted = slot * 16 + lax.broadcasted_iota(jnp.int32, (16, 512), 0)
    one_hot = jnp.where(lax.broadcasted_iota(jnp.int32, (16, 512), 1) == wanted, 1.0, 0.0)
    target_mine = dot(one_hot.astype(BF16), target[...], NT)

    arrived(w_all.at[pl.ds(0, N - 1)], W_G)

    def half_of(ref, c):
        return ref[pl.ds(c * 8, 8)].reshape(256, 256)

    out_send[...] = dot(half_of(w_all, other), act[...], NT).astype(BF16)
    to_twin(out_send, out_c, OUT_C)
    own = dot(half_of(w_all, core), act[...], NT)
    arrived(out_c, OUT_C)
    out_half[...] = (own + out_c[...].astype(F32)).astype(BF16).reshape(N, 16, 1024)
    scatter(out_half, out_recv, OUT_R, False)

    arrived(u_recv, U_R)
    u_part[me] = total(u_send[me], u_recv)
    spread(u_part.at[me], u_part.at[me], U_G, True)

    arrived(out_recv, OUT_R)
    og_all[slot] = (total(out_half[chip], out_recv) - target_mine).astype(BF16)
    spread(og_all.at[slot], og_all.at[slot], OG_G, False)
    arrived(u_part.at[pl.ds(0, N - 1)], U_G)
    u_all[slot] = jnp.concatenate(
        [
            jnp.concatenate([u_part[8 * h + b] for b in range(4)], axis=1)
            for h in range(2)
        ],
        axis=0,
    ).astype(BF16)
    arrived(og_all.at[pl.ds(0, N - 1)], OG_G)
    og_half = og_all.at[pl.ds(core * N, N)]
    to_twin(og_half, og_half, OG_C)

    def g_part(c):
        og = og_all[pl.ds(c * N, N)].reshape(256, 1024)
        g_send[pl.ds(c * 8, 8)] = dot(og, act[...]).astype(BF16).reshape(8, 32, 256)

    g_part(core)
    arrived(og_all.at[pl.ds(0, N)], OG_C)
    g_part(other)
    scatter(g_send, g_recv, G_R, True)
    spread(u_all.at[slot], u_all.at[slot], UD_G, False)
    arrived(g_recv, G_R)
    g_all[me] = total(g_send[me], g_recv).astype(BF16)
    spread(g_all.at[me], g_all.at[me], G_G, True)
    s_full = st[...].T
    s_high = s_full.astype(BF16)
    s_low = (s_full - s_high.astype(F32)).astype(BF16)
    arrived(u_all.at[pl.ds(0, N - 1)], UD_G)
    u_half = u_all.at[pl.ds(core * N, N)]
    to_twin(u_half, u_half, UD_C)
    arrived(g_all.at[pl.ds(0, N - 1)], G_G)

    v_send[...] = dot(half_of(g_all, other), rb[...], NT).astype(BF16)
    to_twin(v_send, v_c, V_C)
    own = dot(half_of(g_all, core), rb[...], NT)
    arrived(v_c, V_C)
    v_half[...] = (own + v_c[...].astype(F32)).astype(BF16).reshape(N, 16, 512)
    scatter(v_half, v_recv, V_R, False)

    g_full = g_all[...].reshape(512, 256)
    grad = dot(s_high, g_full) + dot(s_low, g_full)
    grad_out[...] = grad
    square = jnp.sum((grad * grad).reshape(64, 8, 256), axis=0)
    sq[...] = square[:, :128] + square[:, 128:]
    to_twin(sq, sq_c, SQ_C)

    arrived(v_recv, V_R)
    v_all[slot] = total(v_half[chip], v_recv).astype(BF16)
    spread(v_all.at[slot], v_all.at[slot], V_G, False)
    arrived(sq_c, SQ_C)
    sq_d[0] = sq[...] + sq_c[...]
    each(lambda k: start(sq_d.at[0], sq_d.at[k], SQ_D, chip_dev(k)))
    arrived(v_all.at[pl.ds(0, N - 1)], V_G)
    v_own = v_all.at[pl.ds(core * N, N)]
    to_twin(v_own, v_own, VC_C)

    def p_part(c):
        vt = v_all[pl.ds(c * N, N)].reshape(256, 512)
        p_send[pl.ds(c * 8, 8)] = dot(vt, rb[...]).astype(BF16).reshape(8, 32, 256)

    p_part(core)
    arrived(v_all.at[pl.ds(0, N)], VC_C)
    p_part(other)
    scatter(p_send, p_recv, P_R, True)

    vt = v_all[...].reshape(512, 512)
    v_mine = v_all[slot]
    for part, right in enumerate((vt, st[...].astype(BF16))):
        gram = dot(v_mine, right, NT)
        for h in range(2):
            for b in range(4):
                m_send[8 * h + 4 * part + b] = gram[
                    8 * h : 8 * h + 8, 128 * b : 128 * b + 128
                ]
    scatter(m_send, m_recv, M_R, True)
    arrived(sq_d.at[pl.ds(1, N - 1)], SQ_D)
    square = sq_d[0]
    for k in range(1, N):
        square = square + sq_d[k]
    sq_s[0] = square
    each(lambda k: start(sq_s.at[0], sq_s.at[k], SQ_S, shard_dev(k)))
    arrived(m_recv, M_R)
    m_part[me] = total(m_send[me], m_recv)
    spread(m_part.at[me], m_part.at[me], M_G, True)
    arrived(m_part.at[pl.ds(0, N - 1)], M_G)
    m_all[slot] = jnp.concatenate(
        [
            jnp.concatenate([m_part[8 * h + b] for b in range(8)], axis=1)
            for h in range(2)
        ],
        axis=0,
    ).astype(BF16)
    spread(m_all.at[slot], m_all.at[slot], MD_G, False)
    arrived(p_recv, P_R)
    p_all[me] = total(p_send[me], p_recv).astype(BF16)
    spread(p_all.at[me], p_all.at[me], P_G, True)

    arrived(sq_s.at[pl.ds(1, N - 1)], SQ_S)
    for k in range(1, N):
        square = square + sq_s[k]
    square = jnp.sum(jnp.sum(square, axis=1, keepdims=True), axis=0, keepdims=True)
    step = 0.4 * math.sqrt(512) * lax.rsqrt(D * square + 1e-06)
    arrived(u_all.at[pl.ds(0, N)], UD_C)
    arrived(q_all.at[pl.ds(0, N - 1)], Q_G)
    q_full = q_all[...].reshape(512, 256)
    uu = u_all[...].reshape(512, 512)

    arrived(m_all.at[pl.ds(0, N - 1)], MD_G)
    m_half = m_all.at[pl.ds(core * N, N)]
    to_twin(m_half, m_half, MD_C)
    arrived(p_all.at[pl.ds(0, N - 1)], P_G)
    p_full = p_all[...].reshape(512, 256)
    arrived(m_all.at[pl.ds(0, N)], MD_C)
    m_full = m_all[...].reshape(512, 1024)
    vv, vu = m_full[:, :512], m_full[:, 512:]
    left = 2.0 * p_full.astype(F32) - step * (dot(vu, p_full) - dot(vv, q_full))
    right = 2.0 * q_full.astype(F32) - step * (dot(uu, p_full) - dot(vu, q_full, TN))
    applied = dot(s_high, left.astype(BF16)) - dot(vt, right.astype(BF16), TN)
    next_out[...] = rot[...] - 0.5 * step * applied

    for ref, which in sent:
        pltpu.make_async_copy(ref, ref, sends.at[which]).wait()


def shards(residual, norm_gain, value_weight, rotation, target):
    vmem = pl.BlockSpec(memory_space=pltpu.VMEM)
    scratch = [
        ((512, 512), F32),
        ((512, 256), BF16),
        ((1024, 256), BF16),
        ((16, 128), F32), ((16, 128), F32), ((N, 16, 128), F32),
        ((N, 32, 256), F32), ((N - 1, 32, 256), F32), ((N, 32, 256), BF16), ((N, 32, 256), BF16),
        ((8, 128), F32), ((8, 128), F32), ((N, 8, 128), F32),
        ((256, 1024), BF16), ((256, 1024), BF16), ((N, 16, 1024), BF16), ((N - 1, 16, 1024), BF16),
        ((2 * N, 16, 1024), BF16),
        ((N, 32, 256), BF16), ((N - 1, 32, 256), BF16), ((N, 32, 256), BF16),
        ((256, 512), BF16), ((256, 512), BF16), ((N, 16, 512), BF16), ((N - 1, 16, 512), BF16),
        ((2 * N, 16, 512), BF16),
        ((N, 32, 256), BF16), ((N - 1, 32, 256), BF16), ((N, 32, 256), BF16),
        ((8, 128), F32), ((8, 128), F32), ((N, 8, 128), F32), ((N, 8, 128), F32),
        ((N, 8, 128), F32), ((N - 1, 8, 128), F32), ((N, 8, 128), F32), ((2 * N, 16, 512), BF16),
        ((N, 8, 128), F32), ((N - 1, 8, 128), F32), ((N, 8, 128), F32), ((2 * N, 16, 1024), BF16),
    ]
    return pl.pallas_call(
        kernel,
        out_shape=[jax.ShapeDtypeStruct((512, 256), F32)] * 2,
        in_specs=[vmem] * 5,
        out_specs=[vmem] * 2,
        scratch_shapes=[pltpu.VMEM(shape, kind) for shape, kind in scratch]
        + [pltpu.SemaphoreType.DMA((COUNT,)), pltpu.SemaphoreType.DMA((COUNT,))],
        compiler_params=pltpu.CompilerParams(
            collective_id=0, has_side_effects=True, vmem_limit_bytes=48 * 2**20
        ),
        cost_estimate=pl.CostEstimate(
            flops=2 * 10**9, bytes_accessed=4 * 2**20, transcendentals=0
        ),
    )(residual, norm_gain.reshape(1, -1), value_weight, rotation, target)


def solution(mesh):
    in_specs = (P("shard", "dp"), P("shard"), P("shard", None), P("shard", "dp"), P("shard", None))
    out_specs = (P("shard", "dp"), P("shard", "dp"))
    return jax.shard_map(
        lambda *a: tuple(shards(*a)), mesh=mesh, in_specs=in_specs, out_specs=out_specs, check_vma=False
    )
```

time: 1190 us -> 169 us (0.14)
  waiting for transfers between devices: 894 us -> 0 us
  blocking collectives: 225 us -> 0 us
  Pallas kernels: 0 us -> 160 us
  matrix products: 41.5 us -> 0 us
  between operations: 14.9 us -> 0.65 us
    psum x5 -> x0, waiting for transfers between devices: 709 us -> none  [the longest x1 240 us: shards(): rotated_grad = lax.psum(grad_part, 'dp')]
    psum x2 -> x0, blocking collectives: 161 us -> none  [the longest x1 101 us: shards(): grad_square = lax.psum(local_norm, ('dp', 'shard'))]
    pallas_call x0 -> x1, Pallas kernels: none -> 160 us  [shards(): pl.pallas_call(kernel, out_shape=[jax.ShapeDtypeStruct((512, 256), F32)]...]
    reduce_scatter x1 -> x0, waiting for transfers between devices: 116 us -> none  [shards(): lax.psum_scatter(jnp.dot(rows_block, weight_quant, preferred_element_type...]
    all_gather x1 -> x0, waiting for transfers between devices: 68.9 us -> none  [shards(): lax.all_gather(out_grad, 'dp', axis=0, tiled=True)]
    pmax x1 -> x0, blocking collectives: 63.8 us -> none  [shards(): column_peak = lax.pmax(jnp.max(jnp.abs(rotated), axis=0), 'dp')]
    dot_general x12 -> x0, matrix products: 41.5 us -> none  [the longest x1 8.13 us: shards(): jnp.dot(rows_block, weight_quant, preferred_element_type=jnp.float32)]
  transfers between devices with their start and end apart: 7 -> 0, of which waited for: 7 -> 0; matrix products, arithmetic and copies ran while one was open for 0% -> 0% of each run, Pallas kernels for 0% -> 0%
where the time goes in v1:
time: 169 us; the launch traced here: 168 us
  Pallas kernels  160 us (95%)
  local copies, waits for them, and re-layouts  6.61 us (4%)
    pallas_call x1, Pallas kernels, shards(): pl.pallas_call(kernel, out_shape=[jax.ShapeDtypeStruct((512, 256), F32)]...  160 us
    unnamed x12, local copies, waits for them, and re-layouts  6.61 us

profile of v1, /device:TPU:1, one launch (start us, length us, event | category | flops | bytes accessed | tf_op | source)
XLA Modules:
  0.0 167.6 jit_solution(6829065926189814925)
XLA Ops:
  0.6 0.0 copy-start
  0.6 1.2 copy-done
  1.9 0.0 copy-start.1
  1.9 1.0 copy-done.1
  2.9 0.0 copy-start.2
  2.9 1.0 copy-done.2
  3.9 0.0 copy-start.3
  3.9 1.0 copy-done.3
  5.0 0.0 copy-start.4
  5.0 0.7 copy-done.4
  5.7 160.4 %shard_map.68 = (f32[512,256]{1,0:T(8,128)S(1)}, f32[512,256]{1,0:T(8,128)S(1)}) custom-call(bf16[1024,256]{1,0:T(8,128)(2,1)S(1)} %copy-done.1, f32[1,512]{1,0:T(1,128)S(1)} %bitcast.1, bf16[512,512]{1,0:T(8,128)(2,1)S(1)} %copy-done.2, f32[512,256]{1,0:T(8,128)S(1)} %copy-done.3, bf16[1024,512]{1,0:T(8,128)(2,1)S(1)} %copy-done), custom_call_target="tpu_custom_call" | custom-call | flops 2000000000 | bytes 4194304 | tf_op jit(solution)/shard_map/pallas_call | solution.py:374
  166.0 0.8 copy.9
  166.8 0.8 copy.10
Async XLA Ops:
  0.6 1.2 copy-start
  1.9 1.0 copy-start.1
  2.9 1.0 copy-start.2
  3.9 1.0 copy-start.3
  5.0 0.7 copy-start.4

commit v2 on v1

--- a/solution.py
+++ b/solution.py
@@ -47,20 +47,25 @@
 
 
 (
-    STAT_C, STAT_D, Q_R, PEAK_C, PEAK_D, W_G, Q_G, OUT_C, OUT_R, OG_G, OG_C, G_R, G_G, V_C, V_R, V_G, VC_C,
-    P_R, P_G, SQ_C, SQ_D, SQ_S, U_R, U_G, UD_G, UD_C, M_R, M_G, MD_G, MD_C,
-) = range(30)
-COUNT = 30
+    STAT_C, STAT_D, Q_R, PEAK_C, PEAK_D, W_G, Q_G, G_R, G_G,
+    P_R, P_G, SQ_C, SQ_D, SQ_S, U_R, U_G, UD_G, UD_C, M_R, M_G,
+) = range(20)
+OUT, V = 20, 31
+OG, VG, MG = 42, 53, 64
+COUNT = 75
+FAR = (4, 3, 5, 2, 6, 1, 7)
+NEAR = FAR[::-1]
 
 
 def kernel(
-    res, gain, weight, rot, target, grad_out, next_out,
+    res_in, gain_in, weight_in, rot_in, target_in, grad_out, next_out,
+    res, gain, weight, rot, target, inputs,
     st, rb, act, stat, stat_c, stat_d,
     q_send, q_recv, q_all, w_all,
     peak, peak_c, peak_d,
-    out_send, out_c, out_half, out_recv, og_all,
+    out_send, out_c, out_x, out_xr, out_y, out_yr, og_all,
     g_send, g_recv, g_all,
-    v_send, v_c, v_half, v_recv, v_all,
+    v_send, v_c, v_x, v_xr, v_y, v_yr, v_all,
     p_send, p_recv, p_all,
     sq, sq_c, sq_d, sq_s,
     u_send, u_recv, u_part, u_all,
@@ -69,8 +74,25 @@
 ):
     dp, me = lax.axis_index("dp"), lax.axis_index("shard")
     chip, core = lax.div(dp, 2), lax.rem(dp, 2)
-    other = 1 - core
+    y, xl = lax.div(chip, 2), lax.rem(chip, 2)
+    other, xo = 1 - core, 1 - xl
+    slot = core * N + xl * 8 + y
     twin_id = (chip * 2 + other, me)
+    x_id = ((y * 2 + xo) * 2 + core, me)
+
+    loads = []
+    for n, (src, dst) in enumerate(
+        ((weight_in, weight), (rot_in, rot), (gain_in, gain), (res_in, res), (target_in, target))
+    ):
+        rows = src.shape[0]
+        cuts = 4 if rows > 1 else 1
+        for c in range(cuts):
+            part = pl.ds(c * (rows // cuts), rows // cuts)
+            pltpu.make_async_copy(src.at[part], dst.at[part], inputs.at[n]).start()
+        loads.append(pltpu.make_async_copy(src, dst, inputs.at[n]))
+
+    def y_id(k):
+        return ((lax.rem(y + k, 8) * 2 + xl) * 2 + core, me)
 
     def shard_id(k):
         return lax.rem(me + k, N)
@@ -121,6 +143,52 @@
     def to_twin(src, dst, which):
         start(src, dst, which, twin_id)
 
+    def reduce_dp(part, send, from_twin, x_send, x_recv, y_send, y_recv, base, between=None):
+        width = send.shape[2]
+        for n, h in enumerate((xo, xl)):
+            send[n] = part(other, h).astype(BF16)
+            to_twin(send.at[n], from_twin.at[n], base + n)
+        own = [part(core, xo), part(core, xl)]
+        arrived(from_twin.at[0], base)
+        both = own[0] + from_twin[0].astype(F32)
+        x_send[...] = both.astype(BF16).reshape(8, 16, width)
+        for k in FAR + (0,):
+            start(x_send.at[lax.rem(y + k, 8)], x_recv.at[k], base + 2 + k, x_id)
+        arrived(from_twin.at[1], base + 1)
+        both = own[1] + from_twin[1].astype(F32)
+        y_send[...] = both.reshape(8, 16, width)
+        for k in FAR:
+            arrived(x_recv.at[k], base + 2 + k)
+            x_recv[k] = (y_send[lax.rem(y + k, 8)] + x_recv[k].astype(F32)).astype(BF16)
+            start(x_recv.at[k], y_recv.at[k - 1], base + 10, y_id(k))
+        if between is not None:
+            between()
+        arrived(x_recv.at[0], base + 2)
+        acc = y_send[y] + x_recv[0].astype(F32)
+        arrived(y_recv, base + 10)
+        for k in range(7):
+            acc = acc + y_recv[k].astype(F32)
+        return acc
+
+    def gather_own(ref, base):
+        own = ref.at[slot]
+        for k in FAR:
+            start(own, own, base + k, y_id(k))
+        start(own, own, base + 8, x_id)
+        for k in NEAR:
+            block = ref.at[core * N + xl * 8 + lax.rem(y + 8 - k, 8)]
+            arrived(block, base + k)
+            start(block, block, base + 8, x_id)
+        near = ref.at[pl.ds(core * N + xl * 8, 8)]
+        to_twin(near, near, base + 9)
+        far = ref.at[pl.ds(core * N + xo * 8, 8)]
+        arrived(far, base + 8)
+        to_twin(far, far, base + 10)
+
+    def gather_other(ref, base):
+        arrived(ref.at[pl.ds(0, 8)], base + 9)
+        arrived(ref.at[pl.ds(0, 8)], base + 10)
+
     def total(own, recv):
         acc = own.astype(F32)
         for k in range(N - 1):
@@ -136,11 +204,21 @@
 
     each(greet)
 
+    loads[0].wait()
+    loads[2].wait()
     st[...] = weight[...].astype(F32).T * gain[...] * (1.0 / math.sqrt(D))
-    q_send[...] = dot(st[...], rot[...], NN, HIGHEST).reshape(N, 32, 256)
+    loads[1].wait()
+    q = dot(st[...], rot[...], NN, HIGHEST).reshape(N, 32, 256)
+    high = q.astype(BF16)
+    q_send[:, :32] = high
+    high = high.astype(F32)
+    rest = jnp.floor((q - high) * (15 * 256.0) / (jnp.abs(high) + 1e-30) + 0.5)
+    rest = jnp.clip(rest, -7.0, 7.0)
+    q_send[:, 32:] = (rest[:, :16] * 16.0 + rest[:, 16:]).astype(BF16)
     pl.semaphore_wait(barrier, 2 * N - 1)
     scatter(q_send, q_recv, Q_R, True)
 
+    loads[3].wait()
     for k in range(8):
         h = res[128 * k : 128 * k + 128, :].astype(F32)
         a, b = h[:, :128], h[:, 128:]
@@ -150,7 +228,6 @@
         )
     to_twin(stat, stat_c, STAT_C)
     rb[...] = rot[...].astype(BF16)
-    slot = core * N + chip
     stb = st[...].astype(BF16)
     mine = st[pl.ds(pl.multiple_of(slot * 16, 16), 16), :].astype(BF16)
     u_gram = dot(mine, stb, NT)
@@ -169,7 +246,16 @@
     each(lambda k: start(stat_d.at[0], stat_d.at[k], STAT_D, chip_dev(k)))
 
     arrived(q_recv, Q_R)
-    q_mine = total(q_send[me], q_recv)
+
+    def decode(a):
+        high, rest = a[:32].astype(F32), a[32:].astype(F32)
+        upper = jnp.floor(rest * 0.0625 + 0.5)
+        rest = jnp.concatenate([upper, rest - 16.0 * upper], axis=0)
+        return high + rest * (jnp.abs(high) * (1.0 / (15 * 256)))
+
+    q_mine = decode(q_send[me])
+    for k in range(N - 1):
+        q_mine = q_mine + decode(q_recv[k])
     top = jnp.maximum(jnp.abs(q_mine[:, :128]), jnp.abs(q_mine[:, 128:]))
     top = jnp.max(jnp.concatenate([top] * 4, axis=0).T, axis=0, keepdims=True)
     peak[...] = jnp.broadcast_to(top, (8, 128))
@@ -205,29 +291,36 @@
     spread(q_all.at[me], q_all.at[me], Q_G, True)
     scatter(u_send, u_recv, U_R, True)
 
+    loads[4].wait()
     wanted = slot * 16 + lax.broadcasted_iota(jnp.int32, (16, 512), 0)
     one_hot = jnp.where(lax.broadcasted_iota(jnp.int32, (16, 512), 1) == wanted, 1.0, 0.0)
     target_mine = dot(one_hot.astype(BF16), target[...], NT)
 
     arrived(w_all.at[pl.ds(0, N - 1)], W_G)
 
-    def half_of(ref, c):
-        return ref[pl.ds(c * 8, 8)].reshape(256, 256)
-
-    out_send[...] = dot(half_of(w_all, other), act[...], NT).astype(BF16)
-    to_twin(out_send, out_c, OUT_C)
-    own = dot(half_of(w_all, core), act[...], NT)
-    arrived(out_c, OUT_C)
-    out_half[...] = (own + out_c[...].astype(F32)).astype(BF16).reshape(N, 16, 1024)
-    scatter(out_half, out_recv, OUT_R, False)
-
-    arrived(u_recv, U_R)
-    u_part[me] = total(u_send[me], u_recv)
-    spread(u_part.at[me], u_part.at[me], U_G, True)
-
-    arrived(out_recv, OUT_R)
-    og_all[slot] = (total(out_half[chip], out_recv) - target_mine).astype(BF16)
-    spread(og_all.at[slot], og_all.at[slot], OG_G, False)
+    def quarter(ref, c, h):
+        return ref[pl.ds(c * 8 + h * 4, 4)].reshape(128, 256)
+
+    def weight_gram():
+        arrived(u_recv, U_R)
+        u_part[me] = total(u_send[me], u_recv)
+        spread(u_part.at[me], u_part.at[me], U_G, True)
+
+    out_mine = reduce_dp(
+        lambda c, h: dot(quarter(w_all, c, h), act[...], NT),
+        out_send, out_c, out_x, out_xr, out_y, out_yr, OUT, weight_gram,
+    )
+    og_all[slot] = (out_mine - target_mine).astype(BF16)
+    gather_own(og_all, OG)
+
+    def g_part(c):
+        og = og_all[pl.ds(c * N, N)].reshape(256, 1024)
+        g_send[pl.ds(c * 8, 8)] = dot(og, act[...]).astype(BF16).reshape(8, 32, 256)
+
+    g_part(core)
+    gather_other(og_all, OG)
+    g_part(other)
+    scatter(g_send, g_recv, G_R, True)
     arrived(u_part.at[pl.ds(0, N - 1)], U_G)
     u_all[slot] = jnp.concatenate(
         [
@@ -236,18 +329,7 @@
         ],
         axis=0,
     ).astype(BF16)
-    arrived(og_all.at[pl.ds(0, N - 1)], OG_G)
-    og_half = og_all.at[pl.ds(core * N, N)]
-    to_twin(og_half, og_half, OG_C)
-
-    def g_part(c):
-        og = og_all[pl.ds(c * N, N)].reshape(256, 1024)
-        g_send[pl.ds(c * 8, 8)] = dot(og, act[...]).astype(BF16).reshape(8, 32, 256)
-
-    g_part(core)
-    arrived(og_all.at[pl.ds(0, N)], OG_C)
-    g_part(other)
-    scatter(g_send, g_recv, G_R, True)
+
     spread(u_all.at[slot], u_all.at[slot], UD_G, False)
     arrived(g_recv, G_R)
     g_all[me] = total(g_send[me], g_recv).astype(BF16)
@@ -260,38 +342,30 @@
     to_twin(u_half, u_half, UD_C)
     arrived(g_all.at[pl.ds(0, N - 1)], G_G)
 
-    v_send[...] = dot(half_of(g_all, other), rb[...], NT).astype(BF16)
-    to_twin(v_send, v_c, V_C)
-    own = dot(half_of(g_all, core), rb[...], NT)
-    arrived(v_c, V_C)
-    v_half[...] = (own + v_c[...].astype(F32)).astype(BF16).reshape(N, 16, 512)
-    scatter(v_half, v_recv, V_R, False)
-
-    g_full = g_all[...].reshape(512, 256)
-    grad = dot(s_high, g_full) + dot(s_low, g_full)
-    grad_out[...] = grad
-    square = jnp.sum((grad * grad).reshape(64, 8, 256), axis=0)
-    sq[...] = square[:, :128] + square[:, 128:]
-    to_twin(sq, sq_c, SQ_C)
-
-    arrived(v_recv, V_R)
-    v_all[slot] = total(v_half[chip], v_recv).astype(BF16)
-    spread(v_all.at[slot], v_all.at[slot], V_G, False)
+    def gradient():
+        g_full = g_all[...].reshape(512, 256)
+        grad = dot(s_high, g_full) + dot(s_low, g_full)
+        grad_out[...] = grad
+        square = jnp.sum((grad * grad).reshape(64, 8, 256), axis=0)
+        sq[...] = square[:, :128] + square[:, 128:]
+        to_twin(sq, sq_c, SQ_C)
+
+    v_mine = reduce_dp(
+        lambda c, h: dot(quarter(g_all, c, h), rb[...], NT),
+        v_send, v_c, v_x, v_xr, v_y, v_yr, V, gradient,
+    )
+    v_all[slot] = v_mine.astype(BF16)
+    gather_own(v_all, VG)
     arrived(sq_c, SQ_C)
     sq_d[0] = sq[...] + sq_c[...]
     each(lambda k: start(sq_d.at[0], sq_d.at[k], SQ_D, chip_dev(k)))
-    arrived(v_all.at[pl.ds(0, N - 1)], V_G)
-    v_own = v_all.at[pl.ds(core * N, N)]
-    to_twin(v_own, v_own, VC_C)
 
     def p_part(c):
         vt = v_all[pl.ds(c * N, N)].reshape(256, 512)
         p_send[pl.ds(c * 8, 8)] = dot(vt, rb[...]).astype(BF16).reshape(8, 32, 256)
 
     p_part(core)
-    arrived(v_all.at[pl.ds(0, N)], VC_C)
-    p_part(other)
-    scatter(p_send, p_recv, P_R, True)
+    gather_other(v_all, VG)
 
     vt = v_all[...].reshape(512, 512)
     v_mine = v_all[slot]
@@ -303,15 +377,20 @@
                     8 * h : 8 * h + 8, 128 * b : 128 * b + 128
                 ]
     scatter(m_send, m_recv, M_R, True)
+    p_part(other)
+    scatter(p_send, p_recv, P_R, True)
+    arrived(m_recv, M_R)
+    m_part[me] = total(m_send[me], m_recv)
+    spread(m_part.at[me], m_part.at[me], M_G, True)
     arrived(sq_d.at[pl.ds(1, N - 1)], SQ_D)
     square = sq_d[0]
     for k in range(1, N):
         square = square + sq_d[k]
     sq_s[0] = square
     each(lambda k: start(sq_s.at[0], sq_s.at[k], SQ_S, shard_dev(k)))
-    arrived(m_recv, M_R)
-    m_part[me] = total(m_send[me], m_recv)
-    spread(m_part.at[me], m_part.at[me], M_G, True)
+    arrived(p_recv, P_R)
+    p_all[me] = total(p_send[me], p_recv).astype(BF16)
+    spread(p_all.at[me], p_all.at[me], P_G, True)
     arrived(m_part.at[pl.ds(0, N - 1)], M_G)
     m_all[slot] = jnp.concatenate(
         [
@@ -320,10 +399,7 @@
         ],
         axis=0,
     ).astype(BF16)
-    spread(m_all.at[slot], m_all.at[slot], MD_G, False)
-    arrived(p_recv, P_R)
-    p_all[me] = total(p_send[me], p_recv).astype(BF16)
-    spread(p_all.at[me], p_all.at[me], P_G, True)
+    gather_own(m_all, MG)
 
     arrived(sq_s.at[pl.ds(1, N - 1)], SQ_S)
     for k in range(1, N):
@@ -335,12 +411,9 @@
     q_full = q_all[...].reshape(512, 256)
     uu = u_all[...].reshape(512, 512)
 
-    arrived(m_all.at[pl.ds(0, N - 1)], MD_G)
-    m_half = m_all.at[pl.ds(core * N, N)]
-    to_twin(m_half, m_half, MD_C)
     arrived(p_all.at[pl.ds(0, N - 1)], P_G)
     p_full = p_all[...].reshape(512, 256)
-    arrived(m_all.at[pl.ds(0, N)], MD_C)
+    gather_other(m_all, MG)
     m_full = m_all[...].reshape(512, 1024)
     vv, vu = m_full[:, :512], m_full[:, 512:]
     left = 2.0 * p_full.astype(F32) - step * (dot(vu, p_full) - dot(vv, q_full))
@@ -355,28 +428,32 @@
 def shards(residual, norm_gain, value_weight, rotation, target):
     vmem = pl.BlockSpec(memory_space=pltpu.VMEM)
     scratch = [
+        ((1024, 256), BF16), ((1, 512), F32), ((512, 512), BF16), ((512, 256), F32), ((1024, 512), BF16),
         ((512, 512), F32),
         ((512, 256), BF16),
         ((1024, 256), BF16),
         ((16, 128), F32), ((16, 128), F32), ((N, 16, 128), F32),
-        ((N, 32, 256), F32), ((N - 1, 32, 256), F32), ((N, 32, 256), BF16), ((N, 32, 256), BF16),
+        ((N, 48, 256), BF16), ((N - 1, 48, 256), BF16), ((N, 32, 256), BF16), ((N, 32, 256), BF16),
         ((8, 128), F32), ((8, 128), F32), ((N, 8, 128), F32),
-        ((256, 1024), BF16), ((256, 1024), BF16), ((N, 16, 1024), BF16), ((N - 1, 16, 1024), BF16),
+        ((2, 128, 1024), BF16), ((2, 128, 1024), BF16), ((8, 16, 1024), BF16), ((8, 16, 1024), BF16),
+        ((8, 16, 1024), F32), ((7, 16, 1024), BF16),
         ((2 * N, 16, 1024), BF16),
         ((N, 32, 256), BF16), ((N - 1, 32, 256), BF16), ((N, 32, 256), BF16),
-        ((256, 512), BF16), ((256, 512), BF16), ((N, 16, 512), BF16), ((N - 1, 16, 512), BF16),
+        ((2, 128, 512), BF16), ((2, 128, 512), BF16), ((8, 16, 512), BF16), ((8, 16, 512), BF16),
+        ((8, 16, 512), F32), ((7, 16, 512), BF16),
         ((2 * N, 16, 512), BF16),
         ((N, 32, 256), BF16), ((N - 1, 32, 256), BF16), ((N, 32, 256), BF16),
         ((8, 128), F32), ((8, 128), F32), ((N, 8, 128), F32), ((N, 8, 128), F32),
         ((N, 8, 128), F32), ((N - 1, 8, 128), F32), ((N, 8, 128), F32), ((2 * N, 16, 512), BF16),
         ((N, 8, 128), F32), ((N - 1, 8, 128), F32), ((N, 8, 128), F32), ((2 * N, 16, 1024), BF16),
     ]
+    buffers = [pltpu.VMEM(shape, kind) for shape, kind in scratch]
     return pl.pallas_call(
         kernel,
         out_shape=[jax.ShapeDtypeStruct((512, 256), F32)] * 2,
-        in_specs=[vmem] * 5,
+        in_specs=[pl.BlockSpec(memory_space=pltpu.HBM)] * 5,
         out_specs=[vmem] * 2,
-        scratch_shapes=[pltpu.VMEM(shape, kind) for shape, kind in scratch]
+        scratch_shapes=buffers[:5] + [pltpu.SemaphoreType.DMA((5,))] + buffers[5:]
         + [pltpu.SemaphoreType.DMA((COUNT,)), pltpu.SemaphoreType.DMA((COUNT,))],
         compiler_params=pltpu.CompilerParams(
             collective_id=0, has_side_effects=True, vmem_limit_bytes=48 * 2**20

time: 169 us -> 155 us (0.917)
  Pallas kernels: 160 us -> 148 us
    pallas_call x1, Pallas kernels: 160 us -> 148 us  [shards(): pl.pallas_call(kernel, out_shape=[jax.ShapeDtypeStruct((512, 256), F32)]...]
where the time goes in v2:
time: 155 us
  Pallas kernels  148 us (95%)
  local copies, waits for them, and re-layouts  6.61 us (4%)
    pallas_call x1, Pallas kernels, shards(): pl.pallas_call(kernel, out_shape=[jax.ShapeDtypeStruct((512, 256), F32)]...  148 us
    unnamed x12, local copies, waits for them, and re-layouts  6.61 us

profile of v2, /device:TPU:1, one launch (start us, length us, event | category | flops | bytes accessed | tf_op | source)
XLA Modules:
  0.0 155.0 jit_solution(14459579157266345752)
XLA Ops:
  0.6 0.0 copy-start
  0.6 1.2 copy-done
  1.9 0.0 copy-start.1
  1.9 1.0 copy-done.1
  2.9 0.0 copy-start.2
  2.9 1.0 copy-done.2
  3.9 0.0 copy-start.3
  3.9 1.0 copy-done.3
  5.0 0.0 copy-start.4
  5.0 0.7 copy-done.4
  5.7 147.7 %shard_map.68 = (f32[512,256]{1,0:T(8,128)S(1)}, f32[512,256]{1,0:T(8,128)S(1)}) custom-call(bf16[1024,256]{1,0:T(8,128)(2,1)S(1)} %copy-done.1, f32[1,512]{1,0:T(1,128)S(1)} %bitcast.1, bf16[512,512]{1,0:T(8,128)(2,1)S(1)} %copy-done.2, f32[512,256]{1,0:T(8,128)S(1)} %copy-done.3, bf16[1024,512]{1,0:T(8,128)(2,1)S(1)} %copy-done), custom_call_target="tpu_custom_call" | custom-call | flops 2000000000 | bytes 4194304 | tf_op jit(solution)/shard_map/pallas_call | solution.py:451
  153.4 0.8 copy.9
  154.2 0.8 copy.10
Async XLA Ops:
  0.6 1.2 copy-start
  1.9 1.0 copy-start.1
  2.9 1.0 copy-start.2
  3.9 1.0 copy-start.3
  5.0 0.7 copy-start.4

commit v3 on v2

--- a/solution.py
+++ b/solution.py
@@ -8,6 +8,7 @@
 from jax.sharding import PartitionSpec as P
 
 D = 8192
+LIMIT = 63 * 2**20
 N = 16
 MESH = pl.DeviceIdType.MESH
 F32 = jnp.float32
@@ -47,19 +48,20 @@
 
 
 (
-    STAT_C, STAT_D, Q_R, PEAK_C, PEAK_D, W_G, Q_G, G_R, G_G,
-    P_R, P_G, SQ_C, SQ_D, SQ_S, U_R, U_G, UD_G, UD_C, M_R, M_G,
+    STAT_C, STAT_D, Q_R, PEAK_C, PEAK_D, W_G, Q_G,
+    SQ_C, SQ_D, SQ_S, U_R, U_G, UD_G, UD_C, M_R, M_G, N_R, N_G, ND_G, ND_C,
 ) = range(20)
 OUT, V = 20, 31
 OG, VG, MG = 42, 53, 64
-COUNT = 75
+G_R, G_G, P_R, P_G = 75, 77, 79, 81
+COUNT = 83
 FAR = (4, 3, 5, 2, 6, 1, 7)
 NEAR = FAR[::-1]
 
 
 def kernel(
-    res_in, gain_in, weight_in, rot_in, target_in, grad_out, next_out,
-    res, gain, weight, rot, target, inputs,
+    res_in, gain_in, weight_in, rot_in, target_in, grad_to, next_to,
+    res, gain, weight, rot, target, grad_out, next_out, local,
     st, rb, act, stat, stat_c, stat_d,
     q_send, q_recv, q_all, w_all,
     peak, peak_c, peak_d,
@@ -70,6 +72,7 @@
     sq, sq_c, sq_d, sq_s,
     u_send, u_recv, u_part, u_all,
     m_send, m_recv, m_part, m_all,
+    n_send, n_recv, n_part, n_all,
     sends, recvs,
 ):
     dp, me = lax.axis_index("dp"), lax.axis_index("shard")
@@ -88,8 +91,8 @@
         cuts = 4 if rows > 1 else 1
         for c in range(cuts):
             part = pl.ds(c * (rows // cuts), rows // cuts)
-            pltpu.make_async_copy(src.at[part], dst.at[part], inputs.at[n]).start()
-        loads.append(pltpu.make_async_copy(src, dst, inputs.at[n]))
+            pltpu.make_async_copy(src.at[part], dst.at[part], local.at[n]).start()
+        loads.append(pltpu.make_async_copy(src, dst, local.at[n]))
 
     def y_id(k):
         return ((lax.rem(y + k, 8) * 2 + xl) * 2 + core, me)
@@ -125,30 +128,25 @@
         pltpu.make_async_copy(ref, ref, recvs.at[which]).wait()
         sent.append((ref, which))
 
-    def scatter(src, dst, which, over_shard):
-        def body(k):
-            if over_shard:
-                start(src.at[shard_id(k)], dst.at[k - 1], which, shard_dev(k))
-            else:
-                start(src.at[chip_id(k)], dst.at[k - 1], which, chip_dev(k))
-
-        each(body)
-
-    def spread(ref, dst, which, over_shard):
-        def body(k):
-            start(ref, dst, which, shard_dev(k) if over_shard else chip_dev(k))
-
-        each(body)
+    def scatter(src, dst, which):
+        each(lambda k: start(src.at[shard_id(k)], dst.at[k - 1], which, shard_dev(k)))
+
+    def spread(ref, which, device):
+        each(lambda k: start(ref, ref, which, device(k)))
 
     def to_twin(src, dst, which):
         start(src, dst, which, twin_id)
 
-    def reduce_dp(part, send, from_twin, x_send, x_recv, y_send, y_recv, base, between=None):
+    def reduce_dp(part, send, from_twin, x_send, x_recv, y_send, y_recv, base, between, ready=None):
         width = send.shape[2]
+        if ready is not None:
+            own = [part(core, xo), part(core, xl)]
+            ready()
         for n, h in enumerate((xo, xl)):
             send[n] = part(other, h).astype(BF16)
             to_twin(send.at[n], from_twin.at[n], base + n)
-        own = [part(core, xo), part(core, xl)]
+        if ready is None:
+            own = [part(core, xo), part(core, xl)]
         arrived(from_twin.at[0], base)
         both = own[0] + from_twin[0].astype(F32)
         x_send[...] = both.astype(BF16).reshape(8, 16, width)
@@ -161,8 +159,7 @@
             arrived(x_recv.at[k], base + 2 + k)
             x_recv[k] = (y_send[lax.rem(y + k, 8)] + x_recv[k].astype(F32)).astype(BF16)
             start(x_recv.at[k], y_recv.at[k - 1], base + 10, y_id(k))
-        if between is not None:
-            between()
+        between()
         arrived(x_recv.at[0], base + 2)
         acc = y_send[y] + x_recv[0].astype(F32)
         arrived(y_recv, base + 10)
@@ -170,11 +167,13 @@
             acc = acc + y_recv[k].astype(F32)
         return acc
 
-    def gather_own(ref, base):
+    def gather_own(ref, base, between=None):
         own = ref.at[slot]
         for k in FAR:
             start(own, own, base + k, y_id(k))
         start(own, own, base + 8, x_id)
+        if between is not None:
+            between()
         for k in NEAR:
             block = ref.at[core * N + xl * 8 + lax.rem(y + 8 - k, 8)]
             arrived(block, base + k)
@@ -208,15 +207,16 @@
     loads[2].wait()
     st[...] = weight[...].astype(F32).T * gain[...] * (1.0 / math.sqrt(D))
     loads[1].wait()
-    q = dot(st[...], rot[...], NN, HIGHEST).reshape(N, 32, 256)
+    q = dot(st[...], rot[...], NN, HIGHEST).reshape(2, N, 16, 256)
     high = q.astype(BF16)
-    q_send[:, :32] = high
+    q_send[:, :16] = high[0]
+    q_send[:, 16:32] = high[1]
     high = high.astype(F32)
     rest = jnp.floor((q - high) * (15 * 256.0) / (jnp.abs(high) + 1e-30) + 0.5)
     rest = jnp.clip(rest, -7.0, 7.0)
-    q_send[:, 32:] = (rest[:, :16] * 16.0 + rest[:, 16:]).astype(BF16)
+    q_send[:, 32:] = (rest[0] * 16.0 + rest[1]).astype(BF16)
     pl.semaphore_wait(barrier, 2 * N - 1)
-    scatter(q_send, q_recv, Q_R, True)
+    scatter(q_send, q_recv, Q_R)
 
     loads[3].wait()
     for k in range(8):
@@ -285,26 +285,26 @@
         top = jnp.maximum(top, peak_d[k])
     column = jnp.broadcast_to(top[:1, :], (128, 128)).T[:32, :]
     scale = twin((column + 1e-06) / 7.0)
-    w_all[me] = (scale * soft(q_mine / scale)).astype(BF16)
-    spread(w_all.at[me], w_all.at[me], W_G, True)
-    q_all[me] = q_mine.astype(BF16)
-    spread(q_all.at[me], q_all.at[me], Q_G, True)
-    scatter(u_send, u_recv, U_R, True)
+    w_all[:, me] = (scale * soft(q_mine / scale)).astype(BF16).reshape(2, 16, 256)
+    spread(w_all.at[:, me], W_G, shard_dev)
+    q_all[:, me] = q_mine.astype(BF16).reshape(2, 16, 256)
+    spread(q_all.at[:, me], Q_G, shard_dev)
+    scatter(u_send, u_recv, U_R)
 
     loads[4].wait()
     wanted = slot * 16 + lax.broadcasted_iota(jnp.int32, (16, 512), 0)
     one_hot = jnp.where(lax.broadcasted_iota(jnp.int32, (16, 512), 1) == wanted, 1.0, 0.0)
     target_mine = dot(one_hot.astype(BF16), target[...], NT)
 
-    arrived(w_all.at[pl.ds(0, N - 1)], W_G)
+    arrived(w_all.at[:, pl.ds(0, N - 1)], W_G)
 
     def quarter(ref, c, h):
-        return ref[pl.ds(c * 8 + h * 4, 4)].reshape(128, 256)
+        return ref[c, pl.ds(h * 8, 8)].reshape(128, 256)
 
     def weight_gram():
         arrived(u_recv, U_R)
         u_part[me] = total(u_send[me], u_recv)
-        spread(u_part.at[me], u_part.at[me], U_G, True)
+        spread(u_part.at[me], U_G, shard_dev)
 
     out_mine = reduce_dp(
         lambda c, h: dot(quarter(w_all, c, h), act[...], NT),
@@ -313,150 +313,185 @@
     og_all[slot] = (out_mine - target_mine).astype(BF16)
     gather_own(og_all, OG)
 
+    def send_half(src, dst, which, c):
+        each(lambda k: start(src.at[c, shard_id(k)], dst.at[c, k - 1], which, shard_dev(k)))
+
+    def share_half(src, recv, ref, which, after, c):
+        arrived(recv.at[c], which)
+        acc = src[c, me].astype(F32)
+        for k in range(N - 1):
+            acc = acc + recv[c, k].astype(F32)
+        ref[c, me] = acc.astype(BF16)
+        spread(ref.at[c, me], after, shard_dev)
+
     def g_part(c):
         og = og_all[pl.ds(c * N, N)].reshape(256, 1024)
-        g_send[pl.ds(c * 8, 8)] = dot(og, act[...]).astype(BF16).reshape(8, 32, 256)
+        g_send[c] = dot(og, act[...]).astype(BF16).reshape(N, 16, 256)
 
     g_part(core)
+    send_half(g_send, g_recv, G_R, core)
     gather_other(og_all, OG)
     g_part(other)
-    scatter(g_send, g_recv, G_R, True)
+    send_half(g_send, g_recv, G_R + 1, other)
+
+    def assemble(part, count):
+        rows = [
+            jnp.concatenate([part[8 * h + b] for b in range(count)], axis=1)
+            for h in range(2)
+        ]
+        return jnp.concatenate(rows, axis=0).astype(BF16)
+
+    def to_twin_half(ref, which):
+        half = ref.at[pl.ds(core * N, N)]
+        to_twin(half, half, which)
+
     arrived(u_part.at[pl.ds(0, N - 1)], U_G)
-    u_all[slot] = jnp.concatenate(
-        [
-            jnp.concatenate([u_part[8 * h + b] for b in range(4)], axis=1)
-            for h in range(2)
-        ],
-        axis=0,
-    ).astype(BF16)
-
-    spread(u_all.at[slot], u_all.at[slot], UD_G, False)
-    arrived(g_recv, G_R)
-    g_all[me] = total(g_send[me], g_recv).astype(BF16)
-    spread(g_all.at[me], g_all.at[me], G_G, True)
+    u_all[slot] = assemble(u_part, 4)
+    spread(u_all.at[slot], UD_G, chip_dev)
+    share_half(g_send, g_recv, g_all, G_R, G_G, core)
+    share_half(g_send, g_recv, g_all, G_R + 1, G_G + 1, other)
     s_full = st[...].T
     s_high = s_full.astype(BF16)
     s_low = (s_full - s_high.astype(F32)).astype(BF16)
     arrived(u_all.at[pl.ds(0, N - 1)], UD_G)
-    u_half = u_all.at[pl.ds(core * N, N)]
-    to_twin(u_half, u_half, UD_C)
-    arrived(g_all.at[pl.ds(0, N - 1)], G_G)
+    to_twin_half(u_all, UD_C)
 
     def gradient():
         g_full = g_all[...].reshape(512, 256)
         grad = dot(s_high, g_full) + dot(s_low, g_full)
         grad_out[...] = grad
+        pltpu.make_async_copy(grad_out, grad_to, local.at[5]).start()
         square = jnp.sum((grad * grad).reshape(64, 8, 256), axis=0)
         sq[...] = square[:, :128] + square[:, 128:]
         to_twin(sq, sq_c, SQ_C)
 
+    arrived(g_all.at[0, pl.ds(0, N - 1)], G_G)
     v_mine = reduce_dp(
         lambda c, h: dot(quarter(g_all, c, h), rb[...], NT),
         v_send, v_c, v_x, v_xr, v_y, v_yr, V, gradient,
-    )
-    v_all[slot] = v_mine.astype(BF16)
-    gather_own(v_all, VG)
+        lambda: arrived(g_all.at[0, pl.ds(0, N - 1)], G_G + 1),
+    ).astype(BF16)
+    v_all[slot] = v_mine
+
+    def blocks(ref, gram):
+        for h in range(2):
+            for b in range(8):
+                block = 128 * (b % 4)
+                ref[8 * h + b] = gram[8 * h : 8 * h + 8, block : block + 128]
+
+    def gram_with_weight():
+        blocks(n_send, dot(v_mine, stb, NT))
+        scatter(n_send, n_recv, N_R)
+
+    gather_own(v_all, VG, gram_with_weight)
     arrived(sq_c, SQ_C)
     sq_d[0] = sq[...] + sq_c[...]
     each(lambda k: start(sq_d.at[0], sq_d.at[k], SQ_D, chip_dev(k)))
 
     def p_part(c):
         vt = v_all[pl.ds(c * N, N)].reshape(256, 512)
-        p_send[pl.ds(c * 8, 8)] = dot(vt, rb[...]).astype(BF16).reshape(8, 32, 256)
-
+        p_send[c] = dot(vt, rb[...]).astype(BF16).reshape(N, 16, 256)
+
+    arrived(n_recv, N_R)
+    n_part[me] = total(n_send[me], n_recv)
+    spread(n_part.at[me], N_G, shard_dev)
     p_part(core)
+    send_half(p_send, p_recv, P_R, core)
     gather_other(v_all, VG)
-
     vt = v_all[...].reshape(512, 512)
-    v_mine = v_all[slot]
-    for part, right in enumerate((vt, st[...].astype(BF16))):
-        gram = dot(v_mine, right, NT)
-        for h in range(2):
-            for b in range(4):
-                m_send[8 * h + 4 * part + b] = gram[
-                    8 * h : 8 * h + 8, 128 * b : 128 * b + 128
-                ]
-    scatter(m_send, m_recv, M_R, True)
+    blocks(m_send, dot(v_mine, vt, NT))
+    scatter(m_send, m_recv, M_R)
     p_part(other)
-    scatter(p_send, p_recv, P_R, True)
+    send_half(p_send, p_recv, P_R + 1, other)
+
+    arrived(n_part.at[pl.ds(0, N - 1)], N_G)
+    n_all[slot] = assemble(n_part, 4)
+    spread(n_all.at[slot], ND_G, chip_dev)
     arrived(m_recv, M_R)
     m_part[me] = total(m_send[me], m_recv)
-    spread(m_part.at[me], m_part.at[me], M_G, True)
+    spread(m_part.at[me], M_G, shard_dev)
     arrived(sq_d.at[pl.ds(1, N - 1)], SQ_D)
     square = sq_d[0]
     for k in range(1, N):
         square = square + sq_d[k]
     sq_s[0] = square
     each(lambda k: start(sq_s.at[0], sq_s.at[k], SQ_S, shard_dev(k)))
-    arrived(p_recv, P_R)
-    p_all[me] = total(p_send[me], p_recv).astype(BF16)
-    spread(p_all.at[me], p_all.at[me], P_G, True)
+    share_half(p_send, p_recv, p_all, P_R, P_G, core)
+    v_full = vt.astype(F32).T.astype(BF16)
     arrived(m_part.at[pl.ds(0, N - 1)], M_G)
-    m_all[slot] = jnp.concatenate(
-        [
-            jnp.concatenate([m_part[8 * h + b] for b in range(8)], axis=1)
-            for h in range(2)
-        ],
-        axis=0,
-    ).astype(BF16)
+    m_all[slot] = assemble(m_part, 4)
+    share_half(p_send, p_recv, p_all, P_R + 1, P_G + 1, other)
     gather_own(m_all, MG)
 
+    arrived(n_all.at[pl.ds(0, N - 1)], ND_G)
+    to_twin_half(n_all, ND_C)
     arrived(sq_s.at[pl.ds(1, N - 1)], SQ_S)
     for k in range(1, N):
         square = square + sq_s[k]
     square = jnp.sum(jnp.sum(square, axis=1, keepdims=True), axis=0, keepdims=True)
     step = 0.4 * math.sqrt(512) * lax.rsqrt(D * square + 1e-06)
     arrived(u_all.at[pl.ds(0, N)], UD_C)
-    arrived(q_all.at[pl.ds(0, N - 1)], Q_G)
+    arrived(q_all.at[:, pl.ds(0, N - 1)], Q_G)
     q_full = q_all[...].reshape(512, 256)
     uu = u_all[...].reshape(512, 512)
-
-    arrived(p_all.at[pl.ds(0, N - 1)], P_G)
+    gather_other(m_all, MG)
+    vv = m_all[...].reshape(512, 512)
+    arrived(n_all.at[pl.ds(0, N)], ND_C)
+    vu = n_all[...].reshape(512, 512)
+    left = step * dot(vv, q_full)
+    right = 2.0 * q_full.astype(F32) + step * dot(vu, q_full, TN)
+    arrived(p_all.at[0, pl.ds(0, N - 1)], P_G)
+    arrived(p_all.at[0, pl.ds(0, N - 1)], P_G + 1)
     p_full = p_all[...].reshape(512, 256)
-    gather_other(m_all, MG)
-    m_full = m_all[...].reshape(512, 1024)
-    vv, vu = m_full[:, :512], m_full[:, 512:]
-    left = 2.0 * p_full.astype(F32) - step * (dot(vu, p_full) - dot(vv, q_full))
-    right = 2.0 * q_full.astype(F32) - step * (dot(uu, p_full) - dot(vu, q_full, TN))
-    applied = dot(s_high, left.astype(BF16)) - dot(vt, right.astype(BF16), TN)
-    next_out[...] = rot[...] - 0.5 * step * applied
+    left = left + 2.0 * p_full.astype(F32) - step * dot(vu, p_full)
+    right = right - step * dot(uu, p_full)
+    left, right = left.astype(BF16), right.astype(BF16)
+    for c in range(4):
+        rows = slice(128 * c, 128 * c + 128)
+        applied = dot(s_high[rows], left) - dot(v_full[rows], right)
+        next_out[rows] = rot[rows] - 0.5 * step * applied
+        pltpu.make_async_copy(next_out.at[rows], next_to.at[rows], local.at[6]).start()
 
     for ref, which in sent:
         pltpu.make_async_copy(ref, ref, sends.at[which]).wait()
+    pltpu.make_async_copy(grad_out, grad_to, local.at[5]).wait()
+    pltpu.make_async_copy(next_out, next_to, local.at[6]).wait()
 
 
 def shards(residual, norm_gain, value_weight, rotation, target):
-    vmem = pl.BlockSpec(memory_space=pltpu.VMEM)
+    hbm = pl.BlockSpec(memory_space=pltpu.HBM)
     scratch = [
         ((1024, 256), BF16), ((1, 512), F32), ((512, 512), BF16), ((512, 256), F32), ((1024, 512), BF16),
+        ((512, 256), F32), ((512, 256), F32),
         ((512, 512), F32),
         ((512, 256), BF16),
         ((1024, 256), BF16),
         ((16, 128), F32), ((16, 128), F32), ((N, 16, 128), F32),
-        ((N, 48, 256), BF16), ((N - 1, 48, 256), BF16), ((N, 32, 256), BF16), ((N, 32, 256), BF16),
+        ((N, 48, 256), BF16), ((N - 1, 48, 256), BF16), ((2, N, 16, 256), BF16), ((2, N, 16, 256), BF16),
         ((8, 128), F32), ((8, 128), F32), ((N, 8, 128), F32),
         ((2, 128, 1024), BF16), ((2, 128, 1024), BF16), ((8, 16, 1024), BF16), ((8, 16, 1024), BF16),
         ((8, 16, 1024), F32), ((7, 16, 1024), BF16),
         ((2 * N, 16, 1024), BF16),
-        ((N, 32, 256), BF16), ((N - 1, 32, 256), BF16), ((N, 32, 256), BF16),
+        ((2, N, 16, 256), BF16), ((2, N - 1, 16, 256), BF16), ((2, N, 16, 256), BF16),
         ((2, 128, 512), BF16), ((2, 128, 512), BF16), ((8, 16, 512), BF16), ((8, 16, 512), BF16),
         ((8, 16, 512), F32), ((7, 16, 512), BF16),
         ((2 * N, 16, 512), BF16),
-        ((N, 32, 256), BF16), ((N - 1, 32, 256), BF16), ((N, 32, 256), BF16),
+        ((2, N, 16, 256), BF16), ((2, N - 1, 16, 256), BF16), ((2, N, 16, 256), BF16),
         ((8, 128), F32), ((8, 128), F32), ((N, 8, 128), F32), ((N, 8, 128), F32),
         ((N, 8, 128), F32), ((N - 1, 8, 128), F32), ((N, 8, 128), F32), ((2 * N, 16, 512), BF16),
-        ((N, 8, 128), F32), ((N - 1, 8, 128), F32), ((N, 8, 128), F32), ((2 * N, 16, 1024), BF16),
+        ((N, 8, 128), F32), ((N - 1, 8, 128), F32), ((N, 8, 128), F32), ((2 * N, 16, 512), BF16),
+        ((N, 8, 128), F32), ((N - 1, 8, 128), F32), ((N, 8, 128), F32), ((2 * N, 16, 512), BF16),
     ]
     buffers = [pltpu.VMEM(shape, kind) for shape, kind in scratch]
     return pl.pallas_call(
         kernel,
         out_shape=[jax.ShapeDtypeStruct((512, 256), F32)] * 2,
-        in_specs=[pl.BlockSpec(memory_space=pltpu.HBM)] * 5,
-        out_specs=[vmem] * 2,
-        scratch_shapes=buffers[:5] + [pltpu.SemaphoreType.DMA((5,))] + buffers[5:]
+        in_specs=[hbm] * 5,
+        out_specs=[hbm] * 2,
+        scratch_shapes=buffers[:7] + [pltpu.SemaphoreType.DMA((7,))] + buffers[7:]
         + [pltpu.SemaphoreType.DMA((COUNT,)), pltpu.SemaphoreType.DMA((COUNT,))],
         compiler_params=pltpu.CompilerParams(
-            collective_id=0, has_side_effects=True, vmem_limit_bytes=48 * 2**20
+            collective_id=0, has_side_effects=True, vmem_limit_bytes=LIMIT
         ),
         cost_estimate=pl.CostEstimate(
             flops=2 * 10**9, bytes_accessed=4 * 2**20, transcendentals=0

time: 155 us -> 145 us (0.935)
  Pallas kernels: 148 us -> 141 us
  local copies, waits for them, and re-layouts: 6.61 us -> 2.72 us
    pallas_call x1, Pallas kernels: 148 us -> 141 us  [shards(): pl.pallas_call(kernel, out_shape=[jax.ShapeDtypeStruct((512, 256), F32)]...]
    unnamed x12 -> x4, local copies, waits for them, and re-layouts: 6.61 us -> 2.72 us
where the time goes in v3:
time: 145 us; the launch traced here: 144 us
  Pallas kernels  141 us (97%)
  local copies, waits for them, and re-layouts  2.72 us (2%)
    pallas_call x1, Pallas kernels, shards(): pl.pallas_call(kernel, out_shape=[jax.ShapeDtypeStruct((512, 256), F32)]...  141 us

profile of v3, /device:TPU:1, one launch (start us, length us, event | category | flops | bytes accessed | tf_op | source)
XLA Modules:
  0.0 144.0 jit_solution(54165177204206582)
XLA Ops:
  0.6 140.6 %shard_map.68 = (f32[512,256]{1,0:T(8,128)}, f32[512,256]{1,0:T(8,128)}) custom-call(bf16[1024,256]{1,0:T(8,128)(2,1)} %res_in.1, f32[1,512]{1,0:T(1,128)} %bitcast.1, bf16[512,512]{1,0:T(8,128)(2,1)} %weight_in.1, f32[512,256]{1,0:T(8,128)} %rot_in.1, bf16[1024,512]{1,0:T(8,128)(2,1)} %target_in.1), custom_call_target="tpu_custom_call" | custom-call | flops 2000000000 | bytes 4194304 | tf_op jit(solution)/shard_map/pallas_call | solution.py:486
  141.2 0.0 copy-start
  141.3 1.9 %copy.9 = f32[512,256]{1,0:T(8,128)} copy(f32[512,256]{1,0:T(8,128)} %get-tuple-element.4) | data formatting | bytes 1048576
  143.2 0.0 copy-done
  143.2 0.8 copy.10
Async XLA Ops:
  141.2 1.9 %copy-start = (f32[512,256]{1,0:T(8,128)S(1)}, f32[512,256]{1,0:T(8,128)}, u32[]{:S(2)}) copy-start(f32[512,256]{1,0:T(8,128)} %get-tuple-element.5) | copy-start | bytes 1572868

commit v4 on v3

--- a/solution.py
+++ b/solution.py
@@ -13,7 +13,6 @@
 MESH = pl.DeviceIdType.MESH
 F32 = jnp.float32
 BF16 = jnp.bfloat16
-HIGHEST = lax.Precision.HIGHEST
 
 SINE = (
     0.9999999944722865,
@@ -30,8 +29,8 @@
 TN = (((0,), (0,)), ((), ()))
 
 
-def dot(a, b, dims=NN, precision=None):
-    return lax.dot_general(a, b, dims, precision=precision, preferred_element_type=F32)
+def dot(a, b, dims=NN):
+    return lax.dot_general(a, b, dims, preferred_element_type=F32)
 
 
 def soft(v):
@@ -49,12 +48,13 @@
 
 (
     STAT_C, STAT_D, Q_R, PEAK_C, PEAK_D, W_G, Q_G,
-    SQ_C, SQ_D, SQ_S, U_R, U_G, UD_G, UD_C, M_R, M_G, N_R, N_G, ND_G, ND_C,
-) = range(20)
+    SQ_C, SQ_D, SQ_S, U_R, U_G, UD_G, UD_C, M_R, M_G, N_R, N_G, W_H,
+) = range(19)
 OUT, V = 20, 31
 OG, VG, MG = 42, 53, 64
 G_R, G_G, P_R, P_G = 75, 77, 79, 81
-COUNT = 83
+NG = 83
+COUNT = 94
 FAR = (4, 3, 5, 2, 6, 1, 7)
 NEAR = FAR[::-1]
 
@@ -62,7 +62,7 @@
 def kernel(
     res_in, gain_in, weight_in, rot_in, target_in, grad_to, next_to,
     res, gain, weight, rot, target, grad_out, next_out, local,
-    st, rb, act, stat, stat_c, stat_d,
+    gains, wt, rb, act, stat, stat_c, stat_d,
     q_send, q_recv, q_all, w_all,
     peak, peak_c, peak_d,
     out_send, out_c, out_x, out_xr, out_y, out_yr, og_all,
@@ -137,15 +137,16 @@
     def to_twin(src, dst, which):
         start(src, dst, which, twin_id)
 
-    def reduce_dp(part, send, from_twin, x_send, x_recv, y_send, y_recv, base, between, ready=None):
+    def reduce_dp(part, send, from_twin, x_send, x_recv, y_send, y_recv, base, between, ready, own_first):
         width = send.shape[2]
-        if ready is not None:
+        if own_first:
             own = [part(core, xo), part(core, xl)]
             ready()
         for n, h in enumerate((xo, xl)):
             send[n] = part(other, h).astype(BF16)
             to_twin(send.at[n], from_twin.at[n], base + n)
-        if ready is None:
+        if not own_first:
+            ready()
             own = [part(core, xo), part(core, xl)]
         arrived(from_twin.at[0], base)
         both = own[0] + from_twin[0].astype(F32)
@@ -167,17 +168,19 @@
             acc = acc + y_recv[k].astype(F32)
         return acc
 
-    def gather_own(ref, base, between=None):
+    def gather_y(ref, base):
         own = ref.at[slot]
         for k in FAR:
             start(own, own, base + k, y_id(k))
         start(own, own, base + 8, x_id)
-        if between is not None:
-            between()
+
+    def gather_x(ref, base):
         for k in NEAR:
             block = ref.at[core * N + xl * 8 + lax.rem(y + 8 - k, 8)]
             arrived(block, base + k)
             start(block, block, base + 8, x_id)
+
+    def gather_core(ref, base):
         near = ref.at[pl.ds(core * N + xl * 8, 8)]
         to_twin(near, near, base + 9)
         far = ref.at[pl.ds(core * N + xo * 8, 8)]
@@ -205,9 +208,16 @@
 
     loads[0].wait()
     loads[2].wait()
-    st[...] = weight[...].astype(F32).T * gain[...] * (1.0 / math.sqrt(D))
+    wt[...] = weight[...].astype(F32).T.astype(BF16)
+    norm = gain[...] * (1.0 / math.sqrt(D))
+    for c in range(4):
+        rows = slice(128 * c, 128 * c + 128)
+        gains[rows] = twin(jnp.broadcast_to(norm[:, rows], (128, 128)).T)
     loads[1].wait()
-    q = dot(st[...], rot[...], NN, HIGHEST).reshape(2, N, 16, 256)
+    scaled = rot[...] * gains[...]
+    first = scaled.astype(BF16)
+    second = (scaled - first.astype(F32)).astype(BF16)
+    q = (dot(wt[...], first) + dot(wt[...], second)).reshape(2, N, 16, 256)
     high = q.astype(BF16)
     q_send[:, :16] = high[0]
     q_send[:, 16:32] = high[1]
@@ -228,9 +238,9 @@
         )
     to_twin(stat, stat_c, STAT_C)
     rb[...] = rot[...].astype(BF16)
-    stb = st[...].astype(BF16)
-    mine = st[pl.ds(pl.multiple_of(slot * 16, 16), 16), :].astype(BF16)
-    u_gram = dot(mine, stb, NT)
+    stb = (wt[...].astype(F32) * norm).astype(BF16)
+    mine = wt[pl.ds(pl.multiple_of(slot * 16, 16), 16), :].astype(F32) * norm
+    u_gram = dot(mine.astype(BF16), stb, NT)
     for h in range(2):
         for b in range(4):
             block = u_gram[8 * h : 8 * h + 8, 128 * b : 128 * b + 128]
@@ -286,9 +296,9 @@
     column = jnp.broadcast_to(top[:1, :], (128, 128)).T[:32, :]
     scale = twin((column + 1e-06) / 7.0)
     w_all[:, me] = (scale * soft(q_mine / scale)).astype(BF16).reshape(2, 16, 256)
-    spread(w_all.at[:, me], W_G, shard_dev)
+    spread(w_all.at[other, me], W_G, shard_dev)
+    spread(w_all.at[core, me], W_H, shard_dev)
     q_all[:, me] = q_mine.astype(BF16).reshape(2, 16, 256)
-    spread(q_all.at[:, me], Q_G, shard_dev)
     scatter(u_send, u_recv, U_R)
 
     loads[4].wait()
@@ -296,7 +306,7 @@
     one_hot = jnp.where(lax.broadcasted_iota(jnp.int32, (16, 512), 1) == wanted, 1.0, 0.0)
     target_mine = dot(one_hot.astype(BF16), target[...], NT)
 
-    arrived(w_all.at[:, pl.ds(0, N - 1)], W_G)
+    arrived(w_all.at[0, pl.ds(0, N - 1)], W_G)
 
     def quarter(ref, c, h):
         return ref[c, pl.ds(h * 8, 8)].reshape(128, 256)
@@ -309,9 +319,12 @@
     out_mine = reduce_dp(
         lambda c, h: dot(quarter(w_all, c, h), act[...], NT),
         out_send, out_c, out_x, out_xr, out_y, out_yr, OUT, weight_gram,
+        lambda: arrived(w_all.at[0, pl.ds(0, N - 1)], W_H), False,
     )
     og_all[slot] = (out_mine - target_mine).astype(BF16)
-    gather_own(og_all, OG)
+    gather_y(og_all, OG)
+    gather_x(og_all, OG)
+    gather_core(og_all, OG)
 
     def send_half(src, dst, which, c):
         each(lambda k: start(src.at[c, shard_id(k)], dst.at[c, k - 1], which, shard_dev(k)))
@@ -350,16 +363,15 @@
     spread(u_all.at[slot], UD_G, chip_dev)
     share_half(g_send, g_recv, g_all, G_R, G_G, core)
     share_half(g_send, g_recv, g_all, G_R + 1, G_G + 1, other)
-    s_full = st[...].T
-    s_high = s_full.astype(BF16)
-    s_low = (s_full - s_high.astype(F32)).astype(BF16)
     arrived(u_all.at[pl.ds(0, N - 1)], UD_G)
     to_twin_half(u_all, UD_C)
 
     def gradient():
+        spread(q_all.at[:, me], Q_G, shard_dev)
         g_full = g_all[...].reshape(512, 256)
-        grad = dot(s_high, g_full) + dot(s_low, g_full)
+        grad = dot(weight[...], g_full)
         grad_out[...] = grad
+        grad = grad * gains[...]
         pltpu.make_async_copy(grad_out, grad_to, local.at[5]).start()
         square = jnp.sum((grad * grad).reshape(64, 8, 256), axis=0)
         sq[...] = square[:, :128] + square[:, 128:]
@@ -369,7 +381,7 @@
     v_mine = reduce_dp(
         lambda c, h: dot(quarter(g_all, c, h), rb[...], NT),
         v_send, v_c, v_x, v_xr, v_y, v_yr, V, gradient,
-        lambda: arrived(g_all.at[0, pl.ds(0, N - 1)], G_G + 1),
+        lambda: arrived(g_all.at[0, pl.ds(0, N - 1)], G_G + 1), True,
     ).astype(BF16)
     v_all[slot] = v_mine
 
@@ -379,11 +391,14 @@
                 block = 128 * (b % 4)
                 ref[8 * h + b] = gram[8 * h : 8 * h + 8, block : block + 128]
 
-    def gram_with_weight():
-        blocks(n_send, dot(v_mine, stb, NT))
-        scatter(n_send, n_recv, N_R)
-
-    gather_own(v_all, VG, gram_with_weight)
+    gather_y(v_all, VG)
+    blocks(n_send, dot(v_mine, stb, NT))
+    scatter(n_send, n_recv, N_R)
+    gather_x(v_all, VG)
+    arrived(n_recv, N_R)
+    n_part[me] = total(n_send[me], n_recv)
+    spread(n_part.at[me], N_G, shard_dev)
+    gather_core(v_all, VG)
     arrived(sq_c, SQ_C)
     sq_d[0] = sq[...] + sq_c[...]
     each(lambda k: start(sq_d.at[0], sq_d.at[k], SQ_D, chip_dev(k)))
@@ -392,9 +407,6 @@
         vt = v_all[pl.ds(c * N, N)].reshape(256, 512)
         p_send[c] = dot(vt, rb[...]).astype(BF16).reshape(N, 16, 256)
 
-    arrived(n_recv, N_R)
-    n_part[me] = total(n_send[me], n_recv)
-    spread(n_part.at[me], N_G, shard_dev)
     p_part(core)
     send_half(p_send, p_recv, P_R, core)
     gather_other(v_all, VG)
@@ -406,25 +418,27 @@
 
     arrived(n_part.at[pl.ds(0, N - 1)], N_G)
     n_all[slot] = assemble(n_part, 4)
-    spread(n_all.at[slot], ND_G, chip_dev)
+    gather_y(n_all, NG)
     arrived(m_recv, M_R)
     m_part[me] = total(m_send[me], m_recv)
     spread(m_part.at[me], M_G, shard_dev)
+    share_half(p_send, p_recv, p_all, P_R, P_G, core)
+    gather_x(n_all, NG)
     arrived(sq_d.at[pl.ds(1, N - 1)], SQ_D)
     square = sq_d[0]
     for k in range(1, N):
         square = square + sq_d[k]
     sq_s[0] = square
     each(lambda k: start(sq_s.at[0], sq_s.at[k], SQ_S, shard_dev(k)))
-    share_half(p_send, p_recv, p_all, P_R, P_G, core)
-    v_full = vt.astype(F32).T.astype(BF16)
+    share_half(p_send, p_recv, p_all, P_R + 1, P_G + 1, other)
     arrived(m_part.at[pl.ds(0, N - 1)], M_G)
     m_all[slot] = assemble(m_part, 4)
-    share_half(p_send, p_recv, p_all, P_R + 1, P_G + 1, other)
-    gather_own(m_all, MG)
-
-    arrived(n_all.at[pl.ds(0, N - 1)], ND_G)
-    to_twin_half(n_all, ND_C)
+    gather_y(m_all, MG)
+    gather_core(n_all, NG)
+    v_full = vt.astype(F32).T.astype(BF16)
+    gather_x(m_all, MG)
+    gather_core(m_all, MG)
+
     arrived(sq_s.at[pl.ds(1, N - 1)], SQ_S)
     for k in range(1, N):
         square = square + sq_s[k]
@@ -434,12 +448,12 @@
     arrived(q_all.at[:, pl.ds(0, N - 1)], Q_G)
     q_full = q_all[...].reshape(512, 256)
     uu = u_all[...].reshape(512, 512)
+    gather_other(n_all, NG)
+    vu = n_all[...].reshape(512, 512)
+    right = 2.0 * q_full.astype(F32) + step * dot(vu, q_full, TN)
     gather_other(m_all, MG)
     vv = m_all[...].reshape(512, 512)
-    arrived(n_all.at[pl.ds(0, N)], ND_C)
-    vu = n_all[...].reshape(512, 512)
     left = step * dot(vv, q_full)
-    right = 2.0 * q_full.astype(F32) + step * dot(vu, q_full, TN)
     arrived(p_all.at[0, pl.ds(0, N - 1)], P_G)
     arrived(p_all.at[0, pl.ds(0, N - 1)], P_G + 1)
     p_full = p_all[...].reshape(512, 256)
@@ -448,8 +462,8 @@
     left, right = left.astype(BF16), right.astype(BF16)
     for c in range(4):
         rows = slice(128 * c, 128 * c + 128)
-        applied = dot(s_high[rows], left) - dot(v_full[rows], right)
-        next_out[rows] = rot[rows] - 0.5 * step * applied
+        applied = gains[rows] * dot(weight[rows], left) - dot(v_full[rows], right)
+        next_out[rows] = 0.5 * step * applied
         pltpu.make_async_copy(next_out.at[rows], next_to.at[rows], local.at[6]).start()
 
     for ref, which in sent:
@@ -463,7 +477,8 @@
     scratch = [
         ((1024, 256), BF16), ((1, 512), F32), ((512, 512), BF16), ((512, 256), F32), ((1024, 512), BF16),
         ((512, 256), F32), ((512, 256), F32),
-        ((512, 512), F32),
+        ((512, 256), F32),
+        ((512, 512), BF16),
         ((512, 256), BF16),
         ((1024, 256), BF16),
         ((16, 128), F32), ((16, 128), F32), ((N, 16, 128), F32),
@@ -483,7 +498,7 @@
         ((N, 8, 128), F32), ((N - 1, 8, 128), F32), ((N, 8, 128), F32), ((2 * N, 16, 512), BF16),
     ]
     buffers = [pltpu.VMEM(shape, kind) for shape, kind in scratch]
-    return pl.pallas_call(
+    grad, correction = pl.pallas_call(
         kernel,
         out_shape=[jax.ShapeDtypeStruct((512, 256), F32)] * 2,
         in_specs=[hbm] * 5,
@@ -497,6 +512,7 @@
             flops=2 * 10**9, bytes_accessed=4 * 2**20, transcendentals=0
         ),
     )(residual, norm_gain.reshape(1, -1), value_weight, rotation, target)
+    return grad * (norm_gain * (1.0 / math.sqrt(D)))[:, None], rotation - correction
 
 
 def solution(mesh):

time: 145 us -> 141 us (0.972)
  Pallas kernels: 141 us -> 136 us
  other arithmetic: 0 us -> 3.6 us
  local copies, waits for them, and re-layouts: 2.72 us -> 0.01 us
    pallas_call x1, Pallas kernels: 141 us -> 136 us  [shards(): pl.pallas_call(kernel, out_shape=[jax.ShapeDtypeStruct((512, 256), F32)]...]
    mul x0 -> x2, other arithmetic: none -> 2.74 us  [the longest x1 2.06 us: shards(): grad * (norm_gain * (1.0 / math.sqrt(D)))[:, None]]
    unnamed x4, local copies, waits for them, and re-layouts: 2.72 us -> 0.01 us
where the time goes in v4:
time: 141 us; the launch traced here: 140 us
  Pallas kernels  136 us (96%)
  other arithmetic  3.6 us (3%)
    pallas_call x1, Pallas kernels, shards(): pl.pallas_call(kernel, out_shape=[jax.ShapeDtypeStruct((512, 256), F32)]...  136 us

profile of v4, /device:TPU:1, one launch (start us, length us, event | category | flops | bytes accessed | tf_op | source)
XLA Modules:
  0.0 140.4 jit_solution(11299173154218484716)
XLA Ops:
  0.6 0.7 broadcast_multiply_fusion.1
  1.3 136.2 %shard_map.68 = (f32[512,256]{1,0:T(8,128)}, f32[512,256]{1,0:T(8,128)}) custom-call(bf16[1024,256]{1,0:T(8,128)(2,1)} %res_in.1, f32[1,512]{1,0:T(1,128)} %bitcast.1, bf16[512,512]{1,0:T(8,128)(2,1)} %weight_in.1, f32[512,256]{1,0:T(8,128)} %rot_in.1, bf16[1024,512]{1,0:T(8,128)(2,1)} %target_in.1), custom_call_target="tpu_custom_call" | custom-call | flops 2000000000 | bytes 4194304 | tf_op jit(solution)/shard_map/pallas_call | solution.py:501
  137.5 0.0 copy-start
  137.5 0.0 copy-start.1
  137.5 2.1 %broadcast_multiply_fusion = f32[512,256]{1,0:T(8,128)} fusion(f32[512,256]{1,0:T(8,128)} %get-tuple-element.4, f32[512]{0:T(512)S(1)} %broadcast_multiply_fusion.1), kind=kLoop, calls=%fused_computation | loop fusion | flops 131072 | bytes 1050624 | tf_op jit(solution)/shard_map/mul | solution.py:515
  139.6 0.0 copy-done
  139.6 0.0 copy-done.1
  139.6 0.9 sub.3
Async XLA Ops:
  137.5 2.1 %copy-start = (f32[512,256]{1,0:T(8,128)S(1)}, f32[512,256]{1,0:T(8,128)}, u32[]{:S(2)}) copy-start(f32[512,256]{1,0:T(8,128)} %rot_in.1) | copy-start | bytes 1572868
  137.5 2.1 %copy-start.1 = (f32[512,256]{1,0:T(8,128)S(1)}, f32[512,256]{1,0:T(8,128)}, u32[]{:S(2)}) copy-start(f32[512,256]{1,0:T(8,128)} %get-tuple-element.5) | copy-start | bytes 1572868

commit v5 on v4

--- a/solution.py
+++ b/solution.py
@@ -62,7 +62,7 @@
 def kernel(
     res_in, gain_in, weight_in, rot_in, target_in, grad_to, next_to,
     res, gain, weight, rot, target, grad_out, next_out, local,
-    gains, wt, rb, act, stat, stat_c, stat_d,
+    gains, wt, rb, rb_t, act, act_t, stat, stat_c, stat_d,
     q_send, q_recv, q_all, w_all,
     peak, peak_c, peak_d,
     out_send, out_c, out_x, out_xr, out_y, out_yr, og_all,
@@ -180,15 +180,29 @@
             arrived(block, base + k)
             start(block, block, base + 8, x_id)
 
-    def gather_core(ref, base):
+    def gather_near(ref, base):
         near = ref.at[pl.ds(core * N + xl * 8, 8)]
         to_twin(near, near, base + 9)
+
+    def gather_far(ref, base):
         far = ref.at[pl.ds(core * N + xo * 8, 8)]
         arrived(far, base + 8)
         to_twin(far, far, base + 10)
 
     def gather_other(ref, base):
         arrived(ref.at[pl.ds(0, 8)], base + 9)
+        arrived(ref.at[pl.ds(0, 8)], base + 10)
+
+    def gather_and_send(ref, base, make, src, dst, which):
+        gather_near(ref, base)
+        make(core, xl)
+        send_quarter(src, dst, which, core, xl)
+        gather_far(ref, base)
+        make(core, xo)
+        send_quarter(src, dst, which, core, xo)
+        arrived(ref.at[pl.ds(0, 8)], base + 9)
+        make(other, xl)
+        send_quarter(src, dst, which + 1, other, xl)
         arrived(ref.at[pl.ds(0, 8)], base + 10)
 
     def total(own, recv):
@@ -301,6 +315,8 @@
     q_all[:, me] = q_mine.astype(BF16).reshape(2, 16, 256)
     scatter(u_send, u_recv, U_R)
 
+    act_t[...] = act[...].astype(F32).T.astype(BF16)
+    rb_t[...] = rot[...].T.astype(BF16)
     loads[4].wait()
     wanted = slot * 16 + lax.broadcasted_iota(jnp.int32, (16, 512), 0)
     one_hot = jnp.where(lax.broadcasted_iota(jnp.int32, (16, 512), 1) == wanted, 1.0, 0.0)
@@ -317,17 +333,26 @@
         spread(u_part.at[me], U_G, shard_dev)
 
     out_mine = reduce_dp(
-        lambda c, h: dot(quarter(w_all, c, h), act[...], NT),
+        lambda c, h: dot(quarter(w_all, c, h), act_t[...]),
         out_send, out_c, out_x, out_xr, out_y, out_yr, OUT, weight_gram,
         lambda: arrived(w_all.at[0, pl.ds(0, N - 1)], W_H), False,
     )
     og_all[slot] = (out_mine - target_mine).astype(BF16)
     gather_y(og_all, OG)
     gather_x(og_all, OG)
-    gather_core(og_all, OG)
-
-    def send_half(src, dst, which, c):
-        each(lambda k: start(src.at[c, shard_id(k)], dst.at[c, k - 1], which, shard_dev(k)))
+
+    def send_quarter(src, dst, which, c, h):
+        def step(j, _):
+            to = h * 8 + j
+
+            @pl.when(to != me)
+            def _():
+                k = lax.rem(to + N - me, N)
+                start(src.at[c, to], dst.at[c, k - 1], which, (dp, to))
+
+            return 0
+
+        lax.fori_loop(0, 8, step, 0)
 
     def share_half(src, recv, ref, which, after, c):
         arrived(recv.at[c], which)
@@ -337,15 +362,13 @@
         ref[c, me] = acc.astype(BF16)
         spread(ref.at[c, me], after, shard_dev)
 
-    def g_part(c):
-        og = og_all[pl.ds(c * N, N)].reshape(256, 1024)
-        g_send[c] = dot(og, act[...]).astype(BF16).reshape(N, 16, 256)
-
-    g_part(core)
-    send_half(g_send, g_recv, G_R, core)
-    gather_other(og_all, OG)
-    g_part(other)
-    send_half(g_send, g_recv, G_R + 1, other)
+    def g_part(c, h):
+        og = og_all[pl.ds(c * N + h * 8, 8)].reshape(128, 1024)
+        g_send[c, pl.ds(h * 8, 8)] = dot(og, act[...]).astype(BF16).reshape(8, 16, 256)
+
+    gather_and_send(og_all, OG, g_part, g_send, g_recv, G_R)
+    g_part(other, xo)
+    send_quarter(g_send, g_recv, G_R + 1, other, xo)
 
     def assemble(part, count):
         rows = [
@@ -369,9 +392,8 @@
     def gradient():
         spread(q_all.at[:, me], Q_G, shard_dev)
         g_full = g_all[...].reshape(512, 256)
-        grad = dot(weight[...], g_full)
+        grad = gains[...] * dot(weight[...], g_full)
         grad_out[...] = grad
-        grad = grad * gains[...]
         pltpu.make_async_copy(grad_out, grad_to, local.at[5]).start()
         square = jnp.sum((grad * grad).reshape(64, 8, 256), axis=0)
         sq[...] = square[:, :128] + square[:, 128:]
@@ -379,7 +401,7 @@
 
     arrived(g_all.at[0, pl.ds(0, N - 1)], G_G)
     v_mine = reduce_dp(
-        lambda c, h: dot(quarter(g_all, c, h), rb[...], NT),
+        lambda c, h: dot(quarter(g_all, c, h), rb_t[...]),
         v_send, v_c, v_x, v_xr, v_y, v_yr, V, gradient,
         lambda: arrived(g_all.at[0, pl.ds(0, N - 1)], G_G + 1), True,
     ).astype(BF16)
@@ -398,23 +420,20 @@
     arrived(n_recv, N_R)
     n_part[me] = total(n_send[me], n_recv)
     spread(n_part.at[me], N_G, shard_dev)
-    gather_core(v_all, VG)
+
+    def p_part(c, h):
+        block = v_all[pl.ds(c * N + h * 8, 8)].reshape(128, 512)
+        p_send[c, pl.ds(h * 8, 8)] = dot(block, rb[...]).astype(BF16).reshape(8, 16, 256)
+
+    gather_and_send(v_all, VG, p_part, p_send, p_recv, P_R)
+    vt = v_all[...].reshape(512, 512)
+    blocks(m_send, dot(v_mine, vt, NT))
+    scatter(m_send, m_recv, M_R)
+    p_part(other, xo)
+    send_quarter(p_send, p_recv, P_R + 1, other, xo)
     arrived(sq_c, SQ_C)
     sq_d[0] = sq[...] + sq_c[...]
     each(lambda k: start(sq_d.at[0], sq_d.at[k], SQ_D, chip_dev(k)))
-
-    def p_part(c):
-        vt = v_all[pl.ds(c * N, N)].reshape(256, 512)
-        p_send[c] = dot(vt, rb[...]).astype(BF16).reshape(N, 16, 256)
-
-    p_part(core)
-    send_half(p_send, p_recv, P_R, core)
-    gather_other(v_all, VG)
-    vt = v_all[...].reshape(512, 512)
-    blocks(m_send, dot(v_mine, vt, NT))
-    scatter(m_send, m_recv, M_R)
-    p_part(other)
-    send_half(p_send, p_recv, P_R + 1, other)
 
     arrived(n_part.at[pl.ds(0, N - 1)], N_G)
     n_all[slot] = assemble(n_part, 4)
@@ -434,10 +453,12 @@
     arrived(m_part.at[pl.ds(0, N - 1)], M_G)
     m_all[slot] = assemble(m_part, 4)
     gather_y(m_all, MG)
-    gather_core(n_all, NG)
+    gather_near(n_all, NG)
+    gather_far(n_all, NG)
     v_full = vt.astype(F32).T.astype(BF16)
     gather_x(m_all, MG)
-    gather_core(m_all, MG)
+    gather_near(m_all, MG)
+    gather_far(m_all, MG)
 
     arrived(sq_s.at[pl.ds(1, N - 1)], SQ_S)
     for k in range(1, N):
@@ -463,13 +484,23 @@
     for c in range(4):
         rows = slice(128 * c, 128 * c + 128)
         applied = gains[rows] * dot(weight[rows], left) - dot(v_full[rows], right)
-        next_out[rows] = 0.5 * step * applied
+        next_out[rows] = rot[rows] - 0.5 * step * applied
         pltpu.make_async_copy(next_out.at[rows], next_to.at[rows], local.at[6]).start()
 
     for ref, which in sent:
         pltpu.make_async_copy(ref, ref, sends.at[which]).wait()
     pltpu.make_async_copy(grad_out, grad_to, local.at[5]).wait()
     pltpu.make_async_copy(next_out, next_to, local.at[6]).wait()
+
+
+def hand_over(grad_in, next_in, grad_to, next_to, sems):
+    pairs = ((grad_in, grad_to), (next_in, next_to))
+    for n, (src, dst) in enumerate(pairs):
+        for c in range(8):
+            rows = pl.ds(64 * c, 64)
+            pltpu.make_async_copy(src.at[rows], dst.at[rows], sems.at[n]).start()
+    for n, (src, dst) in enumerate(pairs):
+        pltpu.make_async_copy(src, dst, sems.at[n]).wait()
 
 
 def shards(residual, norm_gain, value_weight, rotation, target):
@@ -479,8 +510,8 @@
         ((512, 256), F32), ((512, 256), F32),
         ((512, 256), F32),
         ((512, 512), BF16),
-        ((512, 256), BF16),
-        ((1024, 256), BF16),
+        ((512, 256), BF16), ((256, 512), BF16),
+        ((1024, 256), BF16), ((256, 1024), BF16),
         ((16, 128), F32), ((16, 128), F32), ((N, 16, 128), F32),
         ((N, 48, 256), BF16), ((N - 1, 48, 256), BF16), ((2, N, 16, 256), BF16), ((2, N, 16, 256), BF16),
         ((8, 128), F32), ((8, 128), F32), ((N, 8, 128), F32),
@@ -498,9 +529,10 @@
         ((N, 8, 128), F32), ((N - 1, 8, 128), F32), ((N, 8, 128), F32), ((2 * N, 16, 512), BF16),
     ]
     buffers = [pltpu.VMEM(shape, kind) for shape, kind in scratch]
-    grad, correction = pl.pallas_call(
+    results = [jax.ShapeDtypeStruct((512, 256), F32)] * 2
+    computed = pl.pallas_call(
         kernel,
-        out_shape=[jax.ShapeDtypeStruct((512, 256), F32)] * 2,
+        out_shape=results,
         in_specs=[hbm] * 5,
         out_specs=[hbm] * 2,
         scratch_shapes=buffers[:7] + [pltpu.SemaphoreType.DMA((7,))] + buffers[7:]
@@ -512,7 +544,15 @@
             flops=2 * 10**9, bytes_accessed=4 * 2**20, transcendentals=0
         ),
     )(residual, norm_gain.reshape(1, -1), value_weight, rotation, target)
-    return grad * (norm_gain * (1.0 / math.sqrt(D)))[:, None], rotation - correction
+    return pl.pallas_call(
+        hand_over,
+        out_shape=results,
+        in_specs=[hbm] * 2,
+        out_specs=[hbm] * 2,
+        scratch_shapes=[pltpu.SemaphoreType.DMA((2,))],
+        compiler_params=pltpu.CompilerParams(vmem_limit_bytes=LIMIT),
+        cost_estimate=pl.CostEstimate(flops=0, bytes_accessed=2 * 2**20, transcendentals=0),
+    )(*computed)
 
 
 def solution(mesh):

time: 141 us -> 170 us (1.21)
  Pallas kernels: 136 us -> 169 us
  other arithmetic: 3.6 us -> 0 us
    pallas_call x1 -> x2, Pallas kernels: 136 us -> 169 us  [the longest x1 136 us: shards(): pl.pallas_call(kernel, out_shape=results, in_specs=[hbm] * 5, out_specs=[...]
    mul x2 -> x0, other arithmetic: 2.74 us -> none  [the longest x1 2.06 us: shards(): grad * (norm_gain * (1.0 / math.sqrt(D)))[:, None]]
where the time goes in v5:
time: 170 us
  Pallas kernels  169 us (99%)
    pallas_call x1, Pallas kernels, shards(): pl.pallas_call(kernel, out_shape=results, in_specs=[hbm] * 5, out_specs=[...  136 us
    pallas_call x1, Pallas kernels, shards(): pl.pallas_call(hand_over, out_shape=results, in_specs=[hbm] * 2, out_spec...  32.9 us

profile of v5, /device:TPU:1, one launch (start us, length us, event | category | flops | bytes accessed | tf_op | source)
XLA Modules:
  0.0 169.6 jit_solution(13547850395735980265)
XLA Ops:
  0.6 136.0 %shard_map.68 = (f32[512,256]{1,0:T(8,128)}, f32[512,256]{1,0:T(8,128)}) custom-call(bf16[1024,256]{1,0:T(8,128)(2,1)} %res_in.1, f32[1,512]{1,0:T(1,128)} %bitcast.1, bf16[512,512]{1,0:T(8,128)(2,1)} %weight_in.1, f32[512,256]{1,0:T(8,128)} %rot_in.1, bf16[1024,512]{1,0:T(8,128)(2,1)} %target_in.1), custom_call_target="tpu_custom_call" | custom-call | flops 2000000000 | bytes 4194304 | tf_op jit(solution)/shard_map/pallas_call | solution.py:533
  136.7 32.9 %shard_map.69 = (f32[512,256]{1,0:T(8,128)}, f32[512,256]{1,0:T(8,128)}) custom-call(f32[512,256]{1,0:T(8,128)} %get-tuple-element.4.grad_in, f32[512,256]{1,0:T(8,128)} %get-tuple-element.5.next_in), custom_call_target="tpu_custom_call" | custom-call | bytes 2097152 | tf_op jit(solution)/shard_map/pallas_call | solution.py:547

commit v6 on v5

--- a/solution.py
+++ b/solution.py
@@ -114,7 +114,7 @@
             body(k)
             return 0
 
-        lax.fori_loop(1, N, step, 0)
+        lax.fori_loop(1, N, step, 0, unroll=True)
 
     def start(src, dst, which, device):
         pltpu.make_async_remote_copy(
@@ -127,6 +127,11 @@
     def arrived(ref, which):
         pltpu.make_async_copy(ref, ref, recvs.at[which]).wait()
         sent.append((ref, which))
+
+    def flush():
+        for ref, which in sent:
+            pltpu.make_async_copy(ref, ref, sends.at[which]).wait()
+        sent.clear()
 
     def scatter(src, dst, which):
         each(lambda k: start(src.at[shard_id(k)], dst.at[k - 1], which, shard_dev(k)))
@@ -352,7 +357,7 @@
 
             return 0
 
-        lax.fori_loop(0, 8, step, 0)
+        lax.fori_loop(0, 8, step, 0, unroll=True)
 
     def share_half(src, recv, ref, which, after, c):
         arrived(recv.at[c], which)
@@ -441,6 +446,7 @@
     arrived(m_recv, M_R)
     m_part[me] = total(m_send[me], m_recv)
     spread(m_part.at[me], M_G, shard_dev)
+    flush()
     share_half(p_send, p_recv, p_all, P_R, P_G, core)
     gather_x(n_all, NG)
     arrived(sq_d.at[pl.ds(1, N - 1)], SQ_D)
@@ -472,6 +478,7 @@
     gather_other(n_all, NG)
     vu = n_all[...].reshape(512, 512)
     right = 2.0 * q_full.astype(F32) + step * dot(vu, q_full, TN)
+    flush()
     gather_other(m_all, MG)
     vv = m_all[...].reshape(512, 512)
     left = step * dot(vv, q_full)
@@ -487,20 +494,31 @@
         next_out[rows] = rot[rows] - 0.5 * step * applied
         pltpu.make_async_copy(next_out.at[rows], next_to.at[rows], local.at[6]).start()
 
-    for ref, which in sent:
-        pltpu.make_async_copy(ref, ref, sends.at[which]).wait()
+    flush()
     pltpu.make_async_copy(grad_out, grad_to, local.at[5]).wait()
     pltpu.make_async_copy(next_out, next_to, local.at[6]).wait()
 
 
-def hand_over(grad_in, next_in, grad_to, next_to, sems):
+def hand_over(grad_in, next_in, grad_to, next_to, held, come, gone):
     pairs = ((grad_in, grad_to), (next_in, next_to))
-    for n, (src, dst) in enumerate(pairs):
-        for c in range(8):
-            rows = pl.ds(64 * c, 64)
-            pltpu.make_async_copy(src.at[rows], dst.at[rows], sems.at[n]).start()
-    for n, (src, dst) in enumerate(pairs):
-        pltpu.make_async_copy(src, dst, sems.at[n]).wait()
+
+    def copies(n, c):
+        rows = pl.ds(128 * c, 128)
+        src, dst = pairs[n]
+        here = held.at[n, rows]
+        return (
+            pltpu.make_async_copy(src.at[rows], here, come.at[n, c]),
+            pltpu.make_async_copy(here, dst.at[rows], gone.at[n, c]),
+        )
+
+    steps = [copies(n, c) for c in range(4) for n in range(2)]
+    for first, _ in steps:
+        first.start()
+    for first, second in steps:
+        first.wait()
+        second.start()
+    for _, second in steps:
+        second.wait()
 
 
 def shards(residual, norm_gain, value_weight, rotation, target):
@@ -549,7 +567,8 @@
         out_shape=results,
         in_specs=[hbm] * 2,
         out_specs=[hbm] * 2,
-        scratch_shapes=[pltpu.SemaphoreType.DMA((2,))],
+        scratch_shapes=[pltpu.VMEM((2, 512, 256), F32)]
+        + [pltpu.SemaphoreType.DMA((2, 4))] * 2,
         compiler_params=pltpu.CompilerParams(vmem_limit_bytes=LIMIT),
         cost_estimate=pl.CostEstimate(flops=0, bytes_accessed=2 * 2**20, transcendentals=0),
     )(*computed)

time: 170 us -> 140 us (0.82)
  Pallas kernels: 169 us -> 139 us
    pallas_call x1, Pallas kernels: 32.9 us -> 2.09 us  [shards(): pl.pallas_call(hand_over, out_shape=results, in_specs=[hbm] * 2, out_spec...]
where the time goes in v6:
time: 140 us; the launch traced here: 139 us
  Pallas kernels  139 us (99%)
    pallas_call x1, Pallas kernels, shards(): pl.pallas_call(kernel, out_shape=results, in_specs=[hbm] * 5, out_specs=[...  137 us

profile of v6, /device:TPU:1, one launch (start us, length us, event | category | flops | bytes accessed | tf_op | source)
XLA Modules:
  0.0 139.4 jit_solution(12695392399737798430)
XLA Ops:
  0.6 136.7 %shard_map.68 = (f32[512,256]{1,0:T(8,128)}, f32[512,256]{1,0:T(8,128)}) custom-call(bf16[1024,256]{1,0:T(8,128)(2,1)} %res_in.1, f32[1,512]{1,0:T(1,128)} %bitcast.1, bf16[512,512]{1,0:T(8,128)(2,1)} %weight_in.1, f32[512,256]{1,0:T(8,128)} %rot_in.1, bf16[1024,512]{1,0:T(8,128)(2,1)} %target_in.1), custom_call_target="tpu_custom_call" | custom-call | flops 2000000000 | bytes 4194304 | tf_op jit(solution)/shard_map/pallas_call | solution.py:551
  137.4 2.1 %shard_map.69 = (f32[512,256]{1,0:T(8,128)}, f32[512,256]{1,0:T(8,128)}) custom-call(f32[512,256]{1,0:T(8,128)} %get-tuple-element.4.grad_in, f32[512,256]{1,0:T(8,128)} %get-tuple-element.5.next_in), custom_call_target="tpu_custom_call" | custom-call | bytes 2097152 | tf_op jit(solution)/shard_map/pallas_call | solution.py:565

commit v7 on v6

--- a/solution.py
+++ b/solution.py
@@ -47,14 +47,15 @@
 
 
 (
-    STAT_C, STAT_D, Q_R, PEAK_C, PEAK_D, W_G, Q_G,
-    SQ_C, SQ_D, SQ_S, U_R, U_G, UD_G, UD_C, M_R, M_G, N_R, N_G, W_H,
-) = range(19)
+    STAT_C, STAT_D, Q_R, PEAK_C, PEAK_D, Q_G,
+    SQ_C, SQ_D, SQ_S, U_R, U_G, UD_G, UD_C, M_R, M_G, N_R, N_G,
+) = range(17)
 OUT, V = 20, 31
 OG, VG, MG = 42, 53, 64
-G_R, G_G, P_R, P_G = 75, 77, 79, 81
+G_R, P_R = 75, 77
 NG = 83
-COUNT = 94
+W_G, G_G, P_G = 94, 110, 126
+COUNT = 142
 FAR = (4, 3, 5, 2, 6, 1, 7)
 NEAR = FAR[::-1]
 
@@ -78,6 +79,7 @@
     dp, me = lax.axis_index("dp"), lax.axis_index("shard")
     chip, core = lax.div(dp, 2), lax.rem(dp, 2)
     y, xl = lax.div(chip, 2), lax.rem(chip, 2)
+    z, xh = lax.div(me, 2), lax.rem(me, 2)
     other, xo = 1 - core, 1 - xl
     slot = core * N + xl * 8 + y
     twin_id = (chip * 2 + other, me)
@@ -210,6 +212,21 @@
         send_quarter(src, dst, which + 1, other, xl)
         arrived(ref.at[pl.ds(0, 8)], base + 10)
 
+    def share(ref, base, c):
+        own = ref.at[c, me]
+        for k in FAR:
+            start(own, own, base + k, (dp, lax.rem(z + k, 8) * 2 + xh))
+        start(own, own, base, (dp, z * 2 + 1 - xh))
+
+    def forward(ref, base, c):
+        for k in NEAR:
+            block = ref.at[c, lax.rem(z + 8 - k, 8) * 2 + xh]
+            arrived(block, base + k)
+            start(block, block, base, (dp, z * 2 + 1 - xh))
+
+    def settled(ref, base):
+        arrived(ref.at[0, pl.ds(0, 8)], base)
+
     def total(own, recv):
         acc = own.astype(F32)
         for k in range(N - 1):
@@ -315,19 +332,21 @@
     column = jnp.broadcast_to(top[:1, :], (128, 128)).T[:32, :]
     scale = twin((column + 1e-06) / 7.0)
     w_all[:, me] = (scale * soft(q_mine / scale)).astype(BF16).reshape(2, 16, 256)
-    spread(w_all.at[other, me], W_G, shard_dev)
-    spread(w_all.at[core, me], W_H, shard_dev)
+    share(w_all, W_G, other)
+    share(w_all, W_G + 8, core)
     q_all[:, me] = q_mine.astype(BF16).reshape(2, 16, 256)
     scatter(u_send, u_recv, U_R)
 
     act_t[...] = act[...].astype(F32).T.astype(BF16)
+    forward(w_all, W_G, other)
     rb_t[...] = rot[...].T.astype(BF16)
     loads[4].wait()
     wanted = slot * 16 + lax.broadcasted_iota(jnp.int32, (16, 512), 0)
     one_hot = jnp.where(lax.broadcasted_iota(jnp.int32, (16, 512), 1) == wanted, 1.0, 0.0)
     target_mine = dot(one_hot.astype(BF16), target[...], NT)
 
-    arrived(w_all.at[0, pl.ds(0, N - 1)], W_G)
+    forward(w_all, W_G + 8, core)
+    settled(w_all, W_G)
 
     def quarter(ref, c, h):
         return ref[c, pl.ds(h * 8, 8)].reshape(128, 256)
@@ -340,7 +359,7 @@
     out_mine = reduce_dp(
         lambda c, h: dot(quarter(w_all, c, h), act_t[...]),
         out_send, out_c, out_x, out_xr, out_y, out_yr, OUT, weight_gram,
-        lambda: arrived(w_all.at[0, pl.ds(0, N - 1)], W_H), False,
+        lambda: settled(w_all, W_G + 8), False,
     )
     og_all[slot] = (out_mine - target_mine).astype(BF16)
     gather_y(og_all, OG)
@@ -365,7 +384,7 @@
         for k in range(N - 1):
             acc = acc + recv[c, k].astype(F32)
         ref[c, me] = acc.astype(BF16)
-        spread(ref.at[c, me], after, shard_dev)
+        share(ref, after, c)
 
     def g_part(c, h):
         og = og_all[pl.ds(c * N + h * 8, 8)].reshape(128, 1024)
@@ -390,7 +409,9 @@
     u_all[slot] = assemble(u_part, 4)
     spread(u_all.at[slot], UD_G, chip_dev)
     share_half(g_send, g_recv, g_all, G_R, G_G, core)
-    share_half(g_send, g_recv, g_all, G_R + 1, G_G + 1, other)
+    share_half(g_send, g_recv, g_all, G_R + 1, G_G + 8, other)
+    forward(g_all, G_G, core)
+    forward(g_all, G_G + 8, other)
     arrived(u_all.at[pl.ds(0, N - 1)], UD_G)
     to_twin_half(u_all, UD_C)
 
@@ -404,11 +425,11 @@
         sq[...] = square[:, :128] + square[:, 128:]
         to_twin(sq, sq_c, SQ_C)
 
-    arrived(g_all.at[0, pl.ds(0, N - 1)], G_G)
+    settled(g_all, G_G)
     v_mine = reduce_dp(
         lambda c, h: dot(quarter(g_all, c, h), rb_t[...]),
         v_send, v_c, v_x, v_xr, v_y, v_yr, V, gradient,
-        lambda: arrived(g_all.at[0, pl.ds(0, N - 1)], G_G + 1), True,
+        lambda: settled(g_all, G_G + 8), True,
     ).astype(BF16)
     v_all[slot] = v_mine
 
@@ -455,10 +476,12 @@
         square = square + sq_d[k]
     sq_s[0] = square
     each(lambda k: start(sq_s.at[0], sq_s.at[k], SQ_S, shard_dev(k)))
-    share_half(p_send, p_recv, p_all, P_R + 1, P_G + 1, other)
+    share_half(p_send, p_recv, p_all, P_R + 1, P_G + 8, other)
+    forward(p_all, P_G, core)
     arrived(m_part.at[pl.ds(0, N - 1)], M_G)
     m_all[slot] = assemble(m_part, 4)
     gather_y(m_all, MG)
+    forward(p_all, P_G + 8, other)
     gather_near(n_all, NG)
     gather_far(n_all, NG)
     v_full = vt.astype(F32).T.astype(BF16)
@@ -482,8 +505,8 @@
     gather_other(m_all, MG)
     vv = m_all[...].reshape(512, 512)
     left = step * dot(vv, q_full)
-    arrived(p_all.at[0, pl.ds(0, N - 1)], P_G)
-    arrived(p_all.at[0, pl.ds(0, N - 1)], P_G + 1)
+    settled(p_all, P_G)
+    settled(p_all, P_G + 8)
     p_full = p_all[...].reshape(512, 256)
     left = left + 2.0 * p_full.astype(F32) - step * dot(vu, p_full)
     right = right - step * dot(uu, p_full)

time: 140 us -> 143 us (1.021)
  Pallas kernels: 139 us -> 142 us
    pallas_call x1, Pallas kernels: 137 us -> 140 us  [shards(): pl.pallas_call(kernel, out_shape=results, in_specs=[hbm] * 5, out_specs=[...]
where the time goes in v7:
time: 143 us
  Pallas kernels  142 us (99%)
    pallas_call x1, Pallas kernels, shards(): pl.pallas_call(kernel, out_shape=results, in_specs=[hbm] * 5, out_specs=[...  140 us

profile of v7, /device:TPU:1, one launch (start us, length us, event | category | flops | bytes accessed | tf_op | source)
XLA Modules:
  0.0 142.6 jit_solution(6771826058989690628)
XLA Ops:
  0.6 139.9 %shard_map.68 = (f32[512,256]{1,0:T(8,128)}, f32[512,256]{1,0:T(8,128)}) custom-call(bf16[1024,256]{1,0:T(8,128)(2,1)} %res_in.1, f32[1,512]{1,0:T(1,128)} %bitcast.1, bf16[512,512]{1,0:T(8,128)(2,1)} %weight_in.1, f32[512,256]{1,0:T(8,128)} %rot_in.1, bf16[1024,512]{1,0:T(8,128)(2,1)} %target_in.1), custom_call_target="tpu_custom_call" | custom-call | flops 2000000000 | bytes 4194304 | tf_op jit(solution)/shard_map/pallas_call | solution.py:574
  140.5 2.1 %shard_map.69 = (f32[512,256]{1,0:T(8,128)}, f32[512,256]{1,0:T(8,128)}) custom-call(f32[512,256]{1,0:T(8,128)} %get-tuple-element.4.grad_in, f32[512,256]{1,0:T(8,128)} %get-tuple-element.5.next_in), custom_call_target="tpu_custom_call" | custom-call | bytes 2097152 | tf_op jit(solution)/shard_map/pallas_call | solution.py:588

commit v8 on v6

--- a/solution.py
+++ b/solution.py
@@ -47,9 +47,9 @@
 
 
 (
-    STAT_C, STAT_D, Q_R, PEAK_C, PEAK_D, W_G, Q_G,
+    STAT_C, STAT_D, Q_R, PEAK_D, W_G, Q_G,
     SQ_C, SQ_D, SQ_S, U_R, U_G, UD_G, UD_C, M_R, M_G, N_R, N_G, W_H,
-) = range(19)
+) = range(18)
 OUT, V = 20, 31
 OG, VG, MG = 42, 53, 64
 G_R, G_G, P_R, P_G = 75, 77, 79, 81
@@ -64,7 +64,7 @@
     res, gain, weight, rot, target, grad_out, next_out, local,
     gains, wt, rb, rb_t, act, act_t, stat, stat_c, stat_d,
     q_send, q_recv, q_all, w_all,
-    peak, peak_c, peak_d,
+    peak, peak_d,
     out_send, out_c, out_x, out_xr, out_y, out_yr, og_all,
     g_send, g_recv, g_all,
     v_send, v_c, v_x, v_xr, v_y, v_yr, v_all,
@@ -185,6 +185,16 @@
             arrived(block, base + k)
             start(block, block, base + 8, x_id)
 
+    def gather_direct(ref, base):
+        own = ref.at[slot]
+        for k in FAR:
+            start(own, own, base + 1, y_id(k))
+        for k in FAR + (0,):
+            start(own, own, base + 8, ((lax.rem(y + k, 8) * 2 + xo) * 2 + core, me))
+
+    def arrived_near(ref, base):
+        arrived(ref.at[pl.ds(0, 7)], base + 1)
+
     def gather_near(ref, base):
         near = ref.at[pl.ds(core * N + xl * 8, 8)]
         to_twin(near, near, base + 9)
@@ -222,6 +232,8 @@
     def greet(k):
         pl.semaphore_signal(barrier, inc=1, device_id=shard_dev(k), device_id_type=MESH)
         pl.semaphore_signal(barrier, inc=1, device_id=chip_dev(k), device_id_type=MESH)
+        there = (chip_id(k) * 2 + other, me)
+        pl.semaphore_signal(barrier, inc=1, device_id=there, device_id_type=MESH)
 
     each(greet)
 
@@ -244,7 +256,7 @@
     rest = jnp.floor((q - high) * (15 * 256.0) / (jnp.abs(high) + 1e-30) + 0.5)
     rest = jnp.clip(rest, -7.0, 7.0)
     q_send[:, 32:] = (rest[0] * 16.0 + rest[1]).astype(BF16)
-    pl.semaphore_wait(barrier, 2 * N - 1)
+    pl.semaphore_wait(barrier, 3 * N - 2)
     scatter(q_send, q_recv, Q_R)
 
     loads[3].wait()
@@ -288,7 +300,11 @@
     top = jnp.maximum(jnp.abs(q_mine[:, :128]), jnp.abs(q_mine[:, 128:]))
     top = jnp.max(jnp.concatenate([top] * 4, axis=0).T, axis=0, keepdims=True)
     peak[...] = jnp.broadcast_to(top, (8, 128))
-    to_twin(peak, peak_c, PEAK_C)
+    row = peak.at[pl.ds(0, 1)]
+    for k in range(N):
+        there = chip_id(k) * 2 + other
+        start(row, peak_d.at[N + k, pl.ds(0, 1)], PEAK_D, (there, me))
+    each(lambda k: start(row, peak_d.at[k, pl.ds(0, 1)], PEAK_D, chip_dev(k)))
 
     arrived(stat_d.at[pl.ds(1, N - 1)], STAT_D)
     for k in range(1, N):
@@ -298,21 +314,16 @@
     rows_in = 7.0 / row_peak
     rows_out = row_peak * inv_rms / 7.0
 
-    arrived(peak_c, PEAK_C)
-    top = jnp.maximum(peak[...], peak_c[...])
-    peak_d[0] = top
-    each(lambda k: start(peak_d.at[0], peak_d.at[k], PEAK_D, chip_dev(k)))
-
     for k in range(8):
         into = twin(jnp.broadcast_to(rows_in[k : k + 1, :], (128, 128)).T)
         outof = twin(jnp.broadcast_to(rows_out[k : k + 1, :], (128, 128)).T)
         h = res[128 * k : 128 * k + 128, :].astype(F32)
         act[128 * k : 128 * k + 128, :] = (outof * soft(into * h)).astype(BF16)
 
-    arrived(peak_d.at[pl.ds(1, N - 1)], PEAK_D)
-    for k in range(1, N):
-        top = jnp.maximum(top, peak_d[k])
-    column = jnp.broadcast_to(top[:1, :], (128, 128)).T[:32, :]
+    arrived(peak_d.at[pl.ds(1, 2 * N - 1), pl.ds(0, 1)], PEAK_D)
+    for k in range(1, 2 * N):
+        top = jnp.maximum(top, peak_d[k, :1, :])
+    column = jnp.broadcast_to(top, (128, 128)).T[:32, :]
     scale = twin((column + 1e-06) / 7.0)
     w_all[:, me] = (scale * soft(q_mine / scale)).astype(BF16).reshape(2, 16, 256)
     spread(w_all.at[other, me], W_G, shard_dev)
@@ -418,10 +429,10 @@
                 block = 128 * (b % 4)
                 ref[8 * h + b] = gram[8 * h : 8 * h + 8, block : block + 128]
 
-    gather_y(v_all, VG)
+    gather_direct(v_all, VG)
     blocks(n_send, dot(v_mine, stb, NT))
     scatter(n_send, n_recv, N_R)
-    gather_x(v_all, VG)
+    arrived_near(v_all, VG)
     arrived(n_recv, N_R)
     n_part[me] = total(n_send[me], n_recv)
     spread(n_part.at[me], N_G, shard_dev)
@@ -442,13 +453,13 @@
 
     arrived(n_part.at[pl.ds(0, N - 1)], N_G)
     n_all[slot] = assemble(n_part, 4)
-    gather_y(n_all, NG)
+    gather_direct(n_all, NG)
     arrived(m_recv, M_R)
     m_part[me] = total(m_send[me], m_recv)
     spread(m_part.at[me], M_G, shard_dev)
     flush()
     share_half(p_send, p_recv, p_all, P_R, P_G, core)
-    gather_x(n_all, NG)
+    arrived_near(n_all, NG)
     arrived(sq_d.at[pl.ds(1, N - 1)], SQ_D)
     square = sq_d[0]
     for k in range(1, N):
@@ -458,11 +469,11 @@
     share_half(p_send, p_recv, p_all, P_R + 1, P_G + 1, other)
     arrived(m_part.at[pl.ds(0, N - 1)], M_G)
     m_all[slot] = assemble(m_part, 4)
-    gather_y(m_all, MG)
+    gather_direct(m_all, MG)
     gather_near(n_all, NG)
     gather_far(n_all, NG)
     v_full = vt.astype(F32).T.astype(BF16)
-    gather_x(m_all, MG)
+    arrived_near(m_all, MG)
     gather_near(m_all, MG)
     gather_far(m_all, MG)
 
@@ -532,7 +543,7 @@
         ((1024, 256), BF16), ((256, 1024), BF16),
         ((16, 128), F32), ((16, 128), F32), ((N, 16, 128), F32),
         ((N, 48, 256), BF16), ((N - 1, 48, 256), BF16), ((2, N, 16, 256), BF16), ((2, N, 16, 256), BF16),
-        ((8, 128), F32), ((8, 128), F32), ((N, 8, 128), F32),
+        ((8, 128), F32), ((2 * N, 8, 128), F32),
         ((2, 128, 1024), BF16), ((2, 128, 1024), BF16), ((8, 16, 1024), BF16), ((8, 16, 1024), BF16),
         ((8, 16, 1024), F32), ((7, 16, 1024), BF16),
         ((2 * N, 16, 1024), BF16),

time: 140 us -> 139 us (level)
  no operation moved by 1% of the time
where the time goes in v8:
time: 139 us; the launch traced here: 138 us
  Pallas kernels  138 us (99%)
    pallas_call x1, Pallas kernels, shards(): pl.pallas_call(kernel, out_shape=results, in_specs=[hbm] * 5, out_specs=[...  136 us

profile of v8, /device:TPU:1, one launch (start us, length us, event | category | flops | bytes accessed | tf_op | source)
XLA Modules:
  0.0 138.4 jit_solution(976061821748546584)
XLA Ops:
  0.6 135.7 %shard_map.68 = (f32[512,256]{1,0:T(8,128)}, f32[512,256]{1,0:T(8,128)}) custom-call(bf16[1024,256]{1,0:T(8,128)(2,1)} %res_in.1, f32[1,512]{1,0:T(1,128)} %bitcast.1, bf16[512,512]{1,0:T(8,128)(2,1)} %weight_in.1, f32[512,256]{1,0:T(8,128)} %rot_in.1, bf16[1024,512]{1,0:T(8,128)(2,1)} %target_in.1), custom_call_target="tpu_custom_call" | custom-call | flops 2000000000 | bytes 4194304 | tf_op jit(solution)/shard_map/pallas_call | solution.py:562
  136.3 2.1 %shard_map.69 = (f32[512,256]{1,0:T(8,128)}, f32[512,256]{1,0:T(8,128)}) custom-call(f32[512,256]{1,0:T(8,128)} %get-tuple-element.4.grad_in, f32[512,256]{1,0:T(8,128)} %get-tuple-element.5.next_in), custom_call_target="tpu_custom_call" | custom-call | bytes 2097152 | tf_op jit(solution)/shard_map/pallas_call | solution.py:576

commit v9 on v8

--- a/solution.py
+++ b/solution.py
@@ -57,6 +57,7 @@
 COUNT = 94
 FAR = (4, 3, 5, 2, 6, 1, 7)
 NEAR = FAR[::-1]
+ORDER = (8, 9, 7, 10, 6, 11, 5, 12, 4, 13, 3, 14, 2, 15, 1)
 
 
 def kernel(
@@ -110,11 +111,8 @@
         return (chip_id(k) * 2 + core, me)
 
     def each(body):
-        def step(k, _):
+        for k in ORDER:
             body(k)
-            return 0
-
-        lax.fori_loop(1, N, step, 0, unroll=True)
 
     def start(src, dst, which, device):
         pltpu.make_async_remote_copy(
@@ -359,7 +357,7 @@
 
     def send_quarter(src, dst, which, c, h):
         def step(j, _):
-            to = h * 8 + j
+            to = h * 8 + lax.rem(me + j, 8)
 
             @pl.when(to != me)
             def _():

time: 139 us -> 134 us (0.964)
  Pallas kernels: 138 us -> 133 us
    pallas_call x1, Pallas kernels: 136 us -> 131 us  [shards(): pl.pallas_call(kernel, out_shape=results, in_specs=[hbm] * 5, out_specs=[...]
where the time goes in v9:
time: 134 us
  Pallas kernels  133 us (99%)
    pallas_call x1, Pallas kernels, shards(): pl.pallas_call(kernel, out_shape=results, in_specs=[hbm] * 5, out_specs=[...  131 us

profile of v9, /device:TPU:1, one launch (start us, length us, event | category | flops | bytes accessed | tf_op | source)
XLA Modules:
  0.0 133.6 jit_solution(16335558618066185092)
XLA Ops:
  0.6 130.9 %shard_map.68 = (f32[512,256]{1,0:T(8,128)}, f32[512,256]{1,0:T(8,128)}) custom-call(bf16[1024,256]{1,0:T(8,128)(2,1)} %res_in.1, f32[1,512]{1,0:T(1,128)} %bitcast.1, bf16[512,512]{1,0:T(8,128)(2,1)} %weight_in.1, f32[512,256]{1,0:T(8,128)} %rot_in.1, bf16[1024,512]{1,0:T(8,128)(2,1)} %target_in.1), custom_call_target="tpu_custom_call" | custom-call | flops 2000000000 | bytes 4194304 | tf_op jit(solution)/shard_map/pallas_call | solution.py:560
  131.5 2.1 %shard_map.69 = (f32[512,256]{1,0:T(8,128)}, f32[512,256]{1,0:T(8,128)}) custom-call(f32[512,256]{1,0:T(8,128)} %get-tuple-element.4.grad_in, f32[512,256]{1,0:T(8,128)} %get-tuple-element.5.next_in), custom_call_target="tpu_custom_call" | custom-call | bytes 2097152 | tf_op jit(solution)/shard_map/pallas_call | solution.py:574
